TPU v7x, 512 devices: a whole 4x8x8 slice. The times are simulated.
512 devices in a mesh: row: 32 (over z, x_hi, core), col: 16 (over x_lo, y).
Axes of the slice: x: 4 (x_hi: 2, x_lo: 2; x = x_hi * 2 + x_lo), y: 8, z: 8, core: 2. Of those that a mesh axis runs over, the one named last changes fastest.
Arguments:
- tokens: bfloat16 [131072, 1024], P(('row', 'col')), may hold values from -6 to 6
- norm_gain: float32 [1024], replicated, may hold values from 0.1 to 1.9
- norm_shift: float32 [1024], replicated, may hold values from -3 to 3
- w_qkv: bfloat16 [1024, 1536], replicated, may hold values from -2 to 13
- links: int32 [512], P(('row', 'col')), may hold values from 0 to 511
Outputs:
- attended: float32 [131072, 512], P(('row', 'col'))
All inputs are finite; a program needn't handle non-finite values.
Results may differ from a plain program's by a relative error of at most 0.014.
The roundings to bfloat16 on the way count: a program that leaves them out, or rounds other values in their place, can miss the bound.
Values may be sent and summed in bfloat16 or wider, within the bound.
No kernel may reach another device: no remote copies, remote signals or barrier semaphores. Data moves between devices by JAX's collectives and lax.ppermute only.
A program may use at most 128 MiB of HBM per device.

v0:
```python
import math

import jax
import jax.numpy as jnp
from jax import lax
from jax.sharding import PartitionSpec as P

HD = 64


def extended(block, sides, width):
    for axis, dim in sides:
        count = lax.axis_size(axis)
        forward = [(i, i + 1) for i in range(count - 1)]
        backward = [(target, source) for source, target in forward]
        low = lax.ppermute(
            lax.slice_in_dim(block, block.shape[dim] - width, None, axis=dim), axis, forward
        )
        high = lax.ppermute(lax.slice_in_dim(block, 0, width, axis=dim), axis, backward)
        block = jnp.concatenate([low, block, high], axis=dim)
    return block


def partner(value, axis, stride):
    mask = 2**stride
    pairs = [(source, source ^ mask) for source in range(lax.axis_size(axis))]
    return lax.ppermute(value, axis, pairs)


def layer_norm(tokens, norm_gain, norm_shift):
    values = tokens.astype(jnp.float32)
    row_mean = jnp.mean(values, axis=-1, keepdims=True)
    centred = values - row_mean
    row_var = jnp.mean(centred * centred, axis=-1, keepdims=True)
    return (centred * lax.rsqrt(row_var + 1e-05) * norm_gain + norm_shift).astype(jnp.bfloat16)


def attend_block(queries, keyval, head_size):
    block_rows, inner = queries.shape
    head_count = inner // head_size
    query_heads = queries.reshape(block_rows, head_count, head_size)
    key_heads = keyval[:, :inner].reshape(-1, head_count, head_size)
    value_heads = keyval[:, inner:].reshape(-1, head_count, head_size)
    scores = jnp.einsum("qhd,khd->hqk", query_heads, key_heads, preferred_element_type=jnp.float32)
    scores = scores * (1.0 / math.sqrt(head_size))
    row_max = jnp.max(scores, axis=-1)
    weights = jnp.exp(scores - row_max[:, :, None])
    row_sum = jnp.sum(weights, axis=-1)
    partial_value = jnp.einsum(
        "hqk,khd->qhd",
        weights.astype(jnp.bfloat16),
        value_heads,
        preferred_element_type=jnp.float32,
    )
    return (partial_value.astype(jnp.bfloat16), row_max, row_sum)


def combine(results, valid_flags):
    valid = jnp.stack(valid_flags)[:, None, None]
    maxima = jnp.stack([entry[1] for entry in results])
    top = jnp.max(jnp.where(valid, maxima, -jnp.inf), axis=0)
    factors = jnp.where(valid, jnp.exp(maxima - top[None]), 0.0)
    sums = jnp.sum(factors * jnp.stack([entry[2] for entry in results]), axis=0)
    block_rows, head_count, head_size = results[0][0].shape
    accum = jnp.zeros((block_rows, head_count, head_size), jnp.float32)
    for index, entry in enumerate(results):
        accum = accum + factors[index].T[:, :, None] * entry[0].astype(jnp.float32)
    return (accum / sums.T[:, :, None]).reshape(block_rows, head_count * head_size)


def per_device(tokens, norm_gain, norm_shift, w_qkv, links):
    normed = layer_norm(tokens, norm_gain, norm_shift)
    projected = jnp.dot(normed, w_qkv, preferred_element_type=jnp.float32).astype(jnp.bfloat16)
    inner = w_qkv.shape[1] // 3
    block_rows = tokens.shape[0]
    queries = projected[:, :inner]
    keyval = projected[:, inner:]
    col_count = lax.axis_size("col")
    row_count = lax.axis_size("row")
    col_index = lax.axis_index("col")
    row_index = lax.axis_index("row")
    block_index = row_index * col_count + col_index
    link_bits = links[0]
    padded = extended(keyval, ((("row", "col"), 0),), block_rows)
    left_block = padded[:block_rows]
    right_block = padded[2 * block_rows :]
    neighbours = [keyval, left_block, right_block]
    valid_flags = [block_index >= 0, block_index > 0, block_index < row_count * col_count - 1]
    col_bits = col_count.bit_length() - 1
    row_bits = row_count.bit_length() - 1
    for section in range(col_bits):
        neighbours.append(partner(keyval, "col", section))
    for section in range(row_bits):
        neighbours.append(partner(keyval, "row", section))
    for section in range(col_bits + row_bits):
        valid_flags.append(jnp.bitwise_and(jnp.right_shift(link_bits, section), 1) == 1)
    results = [attend_block(queries, neighbour, HD) for neighbour in neighbours]
    return combine(results, valid_flags)


def solution(mesh):
    placed = (P(("row", "col"), None), P(), P(), P(), P(("row", "col")))
    return jax.shard_map(
        per_device, mesh=mesh, in_specs=placed, out_specs=P(("row", "col"), None), check_vma=False
    )
```

profile of v0, /device:TPU:1, one launch (start us, length us, event | category | flops | bytes accessed | tf_op | source)
XLA Modules:
  0.0 188.6 jit_solution(3218937935976039934)
XLA Ops:
  2.7 2.1 %convolution_convert_fusion = bf16[256,1536]{1,0:T(8,128)(2,1)S(1)} fusion(bf16[1024,1536]{1,0:T(8,128)(2,1)S(1)} %copy-done, bf16[256,1024]{1,0:T(8,128)(2,1)} %param.5, f32[1024]{0:T(1024)} %param.7, f32[1024]{0:T(1024)} %param.6, f32[256]{0:T(256)S(1)} %add_rsqrt_fusion, f32[256]{0:T(256)S(1)} %broadcast_multiply_fusion), kind=kOutput, calls=%fused_computation | convolution fusion | flops 807272448 | bytes 4466688 | tf_op jit(solution)/shard_map/dot_general | solution.py:73
  5.7 11.5 %collective-permute-start.10 = (bf16[256,1024]{1,0:T(8,128)(2,1)}, bf16[256,1024]{1,0:T(8,128)(2,1)}, u32[]{:S(2)}, u32[]{:S(2)}) collective-permute-start(bf16[256,1024]{1,0:T(8,128)(2,1)} %slice.156), channel_id=1, source_target_pairs={{0,256},{16,272},{32,288},{48,304},{64,320},{80,336},{96,352},{112... | collective-permute-start | bytes 1572872 | tf_op jit(solution)/shard_map/ppermute | solution.py:27
  17.2 4.0 %collective-permute-start.9 = (bf16[256,1024]{1,0:T(8,128)(2,1)}, bf16[256,1024]{1,0:T(8,128)(2,1)}, u32[]{:S(2)}, u32[]{:S(2)}) collective-permute-start(bf16[256,1024]{1,0:T(8,128)(2,1)} %slice.156), channel_id=1, source_target_pairs={{0,128},{16,144},{32,160},{48,176},{64,192},{80,208},{96,224},{112... | collective-permute-start | bytes 1572872 | tf_op jit(solution)/shard_map/ppermute | solution.py:27
  21.2 3.1 %collective-permute-start.8 = (bf16[256,1024]{1,0:T(8,128)(2,1)}, bf16[256,1024]{1,0:T(8,128)(2,1)}, u32[]{:S(2)}, u32[]{:S(2)}) collective-permute-start(bf16[256,1024]{1,0:T(8,128)(2,1)} %slice.156), channel_id=1, source_target_pairs={{0,64},{16,80},{32,96},{48,112},{64,0},{80,16},{96,32},{112,48},{1... | collective-permute-start | bytes 1572872 | tf_op jit(solution)/shard_map/ppermute | solution.py:27
  24.3 4.7 %collective-permute-start.7 = (bf16[256,1024]{1,0:T(8,128)(2,1)}, bf16[256,1024]{1,0:T(8,128)(2,1)}, u32[]{:S(2)}, u32[]{:S(2)}) collective-permute-start(bf16[256,1024]{1,0:T(8,128)(2,1)} %slice.156), channel_id=1, source_target_pairs={{0,32},{16,48},{32,0},{48,16},{64,96},{80,112},{96,64},{112,80},{1... | collective-permute-start | bytes 1572872 | tf_op jit(solution)/shard_map/ppermute | solution.py:27
  28.9 3.7 %collective-permute-start.6 = (bf16[256,1024]{1,0:T(8,128)(2,1)}, bf16[256,1024]{1,0:T(8,128)(2,1)}, u32[]{:S(2)}, u32[]{:S(2)}) collective-permute-start(bf16[256,1024]{1,0:T(8,128)(2,1)} %slice.156), channel_id=1, source_target_pairs={{0,16},{16,0},{32,48},{48,32},{64,80},{80,64},{96,112},{112,96},{1... | collective-permute-start | bytes 1572872 | tf_op jit(solution)/shard_map/ppermute | solution.py:27
  41.8 2.2 %collective-permute-start.5 = (bf16[256,1024]{1,0:T(8,128)(2,1)}, bf16[256,1024]{1,0:T(8,128)(2,1)S(1)}, u32[]{:S(2)}, u32[]{:S(2)}) collective-permute-start(bf16[256,1024]{1,0:T(8,128)(2,1)} %slice.156), channel_id=1, source_target_pairs={{0,8},{1,9},{2,10},{3,11},{4,12},{5,13},{6,14},{7,15},{8,0},{9,1},... | collective-permute-start | bytes 1572872 | tf_op jit(solution)/shard_map/ppermute | solution.py:27
  44.0 1.9 fusion.142
  45.9 18.9 %collective-permute-done.9 = bf16[256,1024]{1,0:T(8,128)(2,1)} collective-permute-done((bf16[256,1024]{1,0:T(8,128)(2,1)}, bf16[256,1024]{1,0:T(8,128)(2,1)}, u32[]{:S(2)}, u32[]{:S(2)}) %collective-permute-start.9) | collective-permute-done | bytes 524320 | tf_op jit(solution)/shard_map/ppermute | solution.py:27
  64.8 7.4 %collective-permute-start.4 = (bf16[256,1024]{1,0:T(8,128)(2,1)}, bf16[256,1024]{1,0:T(8,128)(2,1)S(1)}, u32[]{:S(2)}, u32[]{:S(2)}) collective-permute-start(bf16[256,1024]{1,0:T(8,128)(2,1)} %slice.156), channel_id=1, source_target_pairs={{0,4},{1,5},{2,6},{3,7},{4,0},{5,1},{6,2},{7,3},{8,12},{9,13},{10,... | collective-permute-start | bytes 1572872 | tf_op jit(solution)/shard_map/ppermute | solution.py:27
  72.2 1.9 fusion.141
  74.1 2.4 %collective-permute-start.3 = (bf16[256,1024]{1,0:T(8,128)(2,1)}, bf16[256,1024]{1,0:T(8,128)(2,1)S(1)}, u32[]{:S(2)}, u32[]{:S(2)}) collective-permute-start(bf16[256,1024]{1,0:T(8,128)(2,1)} %slice.156), channel_id=1, source_target_pairs={{0,2},{1,3},{2,0},{3,1},{4,6},{5,7},{6,4},{7,5},{8,10},{9,11},{10,... | collective-permute-start | bytes 1572872 | tf_op jit(solution)/shard_map/ppermute | solution.py:27
  76.5 1.9 fusion.140
  78.4 2.3 %collective-permute-start.2 = (bf16[256,1024]{1,0:T(8,128)(2,1)}, bf16[256,1024]{1,0:T(8,128)(2,1)}, u32[]{:S(2)}, u32[]{:S(2)}) collective-permute-start(bf16[256,1024]{1,0:T(8,128)(2,1)} %slice.156), channel_id=1, source_target_pairs={{0,1},{1,0},{2,3},{3,2},{4,5},{5,4},{6,7},{7,6},{8,9},{9,8},{10,11... | collective-permute-start | bytes 1572872 | tf_op jit(solution)/shard_map/ppermute | solution.py:27
  80.7 1.9 %fusion.139 = (bf16[256,512]{1,0:T(8,128)(2,1)}, bf16[256,512]{1,0:T(8,128)(2,1)}) fusion(bf16[256,1024]{1,0:T(8,128)(2,1)} %collective-permute-done.7), kind=kLoop, calls=%fused_computation.206 | loop fusion | bytes 1048576 | tf_op jit(solution)/shard_map/slice | solution.py:43
  82.6 3.5 %collective-permute-start.1 = (bf16[256,1024]{1,0:T(8,128)(2,1)}, bf16[256,1024]{1,0:T(8,128)(2,1)}, u32[]{:S(2)}, u32[]{:S(2)}) collective-permute-start(bf16[256,1024]{1,0:T(8,128)(2,1)} %slice.156), channel_id=1, source_target_pairs={{1,0},{2,1},{3,2},{4,3},{5,4},{6,5},{7,6},{8,7},{9,8},{10,9},{11,1... | collective-permute-start | bytes 1572872 | tf_op jit(solution)/shard_map/ppermute | solution.py:19
  86.1 1.9 fusion.138
  88.0 2.1 %collective-permute-start = (bf16[256,1024]{1,0:T(8,128)(2,1)}, bf16[256,1024]{1,0:T(8,128)(2,1)}, u32[]{:S(2)}, u32[]{:S(2)}) collective-permute-start(bf16[256,1024]{1,0:T(8,128)(2,1)} %slice.156), channel_id=1, source_target_pairs={{0,1},{1,2},{2,3},{3,4},{4,5},{5,6},{6,7},{7,8},{8,9},{9,10},{10,1... | collective-permute-start | bytes 1572872 | tf_op jit(solution)/shard_map/ppermute | solution.py:16
  91.8 27.5 %collective-permute-done.3 = bf16[256,1024]{1,0:T(8,128)(2,1)S(1)} collective-permute-done((bf16[256,1024]{1,0:T(8,128)(2,1)}, bf16[256,1024]{1,0:T(8,128)(2,1)S(1)}, u32[]{:S(2)}, u32[]{:S(2)}) %collective-permute-start.3) | collective-permute-done | bytes 524320 | tf_op jit(solution)/shard_map/ppermute | solution.py:27
  130.8 1.8 copy.84
  134.4 1.8 copy.82
  136.2 1.8 copy.63
  138.0 1.8 copy.80
  143.4 1.8 copy.61
  145.2 1.8 copy.76
  148.8 1.9 %fusion.134 = (bf16[256,512]{1,0:T(8,128)(2,1)}, bf16[256,512]{1,0:T(8,128)(2,1)}) fusion(bf16[256,1024]{1,0:T(8,128)(2,1)} %collective-permute-done.2), kind=kLoop, calls=%fused_computation.201 | loop fusion | bytes 1048576 | tf_op jit(solution)/shard_map/slice | solution.py:43
  152.5 1.8 copy.59
  154.3 1.9 fusion.133
  157.9 1.8 copy.58
  159.7 1.9 fusion.132
  161.6 1.8 copy.70
  186.6 2.0 %copy.92 = f32[256,512]{1,0:T(8,128)} copy(f32[256,512]{0,1:T(8,128)} %bitcast.247) | data formatting | bytes 1048576 | tf_op jit(solution)/shard_map/reshape | solution.py:68
  (149 shorter events, 58.5 us)
Async XLA Ops:
  0.0 2.7 %copy-start = (bf16[1024,1536]{1,0:T(8,128)(2,1)S(1)}, bf16[1024,1536]{1,0:T(8,128)(2,1)}, u32[]{:S(2)}) copy-start(bf16[1024,1536]{1,0:T(8,128)(2,1)} %param.8) | copy-start | bytes 9437188
  5.7 36.1 %collective-permute-start.10 = (bf16[256,1024]{1,0:T(8,128)(2,1)}, bf16[256,1024]{1,0:T(8,128)(2,1)}, u32[]{:S(2)}, u32[]{:S(2)}) collective-permute-start(bf16[256,1024]{1,0:T(8,128)(2,1)} %slice.156), channel_id=1, source_target_pairs={{0,256},{16,272},{32,288},{48,304},{64,320},{80,336},{96,352},{112... | collective-permute-start | bytes 1572872 | tf_op jit(solution)/shard_map/ppermute | solution.py:27
  17.2 47.6 %collective-permute-start.9 = (bf16[256,1024]{1,0:T(8,128)(2,1)}, bf16[256,1024]{1,0:T(8,128)(2,1)}, u32[]{:S(2)}, u32[]{:S(2)}) collective-permute-start(bf16[256,1024]{1,0:T(8,128)(2,1)} %slice.156), channel_id=1, source_target_pairs={{0,128},{16,144},{32,160},{48,176},{64,192},{80,208},{96,224},{112... | collective-permute-start | bytes 1572872 | tf_op jit(solution)/shard_map/ppermute | solution.py:27
  21.2 52.9 %collective-permute-start.8 = (bf16[256,1024]{1,0:T(8,128)(2,1)}, bf16[256,1024]{1,0:T(8,128)(2,1)}, u32[]{:S(2)}, u32[]{:S(2)}) collective-permute-start(bf16[256,1024]{1,0:T(8,128)(2,1)} %slice.156), channel_id=1, source_target_pairs={{0,64},{16,80},{32,96},{48,112},{64,0},{80,16},{96,32},{112,48},{1... | collective-permute-start | bytes 1572872 | tf_op jit(solution)/shard_map/ppermute | solution.py:27
  24.3 54.1 %collective-permute-start.7 = (bf16[256,1024]{1,0:T(8,128)(2,1)}, bf16[256,1024]{1,0:T(8,128)(2,1)}, u32[]{:S(2)}, u32[]{:S(2)}) collective-permute-start(bf16[256,1024]{1,0:T(8,128)(2,1)} %slice.156), channel_id=1, source_target_pairs={{0,32},{16,48},{32,0},{48,16},{64,96},{80,112},{96,64},{112,80},{1... | collective-permute-start | bytes 1572872 | tf_op jit(solution)/shard_map/ppermute | solution.py:27
  28.9 53.6 %collective-permute-start.6 = (bf16[256,1024]{1,0:T(8,128)(2,1)}, bf16[256,1024]{1,0:T(8,128)(2,1)}, u32[]{:S(2)}, u32[]{:S(2)}) collective-permute-start(bf16[256,1024]{1,0:T(8,128)(2,1)} %slice.156), channel_id=1, source_target_pairs={{0,16},{16,0},{32,48},{48,32},{64,80},{80,64},{96,112},{112,96},{1... | collective-permute-start | bytes 1572872 | tf_op jit(solution)/shard_map/ppermute | solution.py:27
  36.9 1.4 copy-start.1
  41.8 46.2 %collective-permute-start.5 = (bf16[256,1024]{1,0:T(8,128)(2,1)}, bf16[256,1024]{1,0:T(8,128)(2,1)S(1)}, u32[]{:S(2)}, u32[]{:S(2)}) collective-permute-start(bf16[256,1024]{1,0:T(8,128)(2,1)} %slice.156), channel_id=1, source_target_pairs={{0,8},{1,9},{2,10},{3,11},{4,12},{5,13},{6,14},{7,15},{8,0},{9,1},... | collective-permute-start | bytes 1572872 | tf_op jit(solution)/shard_map/ppermute | solution.py:27
  64.8 26.2 %collective-permute-start.4 = (bf16[256,1024]{1,0:T(8,128)(2,1)}, bf16[256,1024]{1,0:T(8,128)(2,1)S(1)}, u32[]{:S(2)}, u32[]{:S(2)}) collective-permute-start(bf16[256,1024]{1,0:T(8,128)(2,1)} %slice.156), channel_id=1, source_target_pairs={{0,4},{1,5},{2,6},{3,7},{4,0},{5,1},{6,2},{7,3},{8,12},{9,13},{10,... | collective-permute-start | bytes 1572872 | tf_op jit(solution)/shard_map/ppermute | solution.py:27
  74.1 45.2 %collective-permute-start.3 = (bf16[256,1024]{1,0:T(8,128)(2,1)}, bf16[256,1024]{1,0:T(8,128)(2,1)S(1)}, u32[]{:S(2)}, u32[]{:S(2)}) collective-permute-start(bf16[256,1024]{1,0:T(8,128)(2,1)} %slice.156), channel_id=1, source_target_pairs={{0,2},{1,3},{2,0},{3,1},{4,6},{5,7},{6,4},{7,5},{8,10},{9,11},{10,... | collective-permute-start | bytes 1572872 | tf_op jit(solution)/shard_map/ppermute | solution.py:27
  78.4 70.4 %collective-permute-start.2 = (bf16[256,1024]{1,0:T(8,128)(2,1)}, bf16[256,1024]{1,0:T(8,128)(2,1)}, u32[]{:S(2)}, u32[]{:S(2)}) collective-permute-start(bf16[256,1024]{1,0:T(8,128)(2,1)} %slice.156), channel_id=1, source_target_pairs={{0,1},{1,0},{2,3},{3,2},{4,5},{5,4},{6,7},{7,6},{8,9},{9,8},{10,11... | collective-permute-start | bytes 1572872 | tf_op jit(solution)/shard_map/ppermute | solution.py:27
  82.6 71.7 %collective-permute-start.1 = (bf16[256,1024]{1,0:T(8,128)(2,1)}, bf16[256,1024]{1,0:T(8,128)(2,1)}, u32[]{:S(2)}, u32[]{:S(2)}) collective-permute-start(bf16[256,1024]{1,0:T(8,128)(2,1)} %slice.156), channel_id=1, source_target_pairs={{1,0},{2,1},{3,2},{4,3},{5,4},{6,5},{7,6},{8,7},{9,8},{10,9},{11,1... | collective-permute-start | bytes 1572872 | tf_op jit(solution)/shard_map/ppermute | solution.py:19
  88.0 71.7 %collective-permute-start = (bf16[256,1024]{1,0:T(8,128)(2,1)}, bf16[256,1024]{1,0:T(8,128)(2,1)}, u32[]{:S(2)}, u32[]{:S(2)}) collective-permute-start(bf16[256,1024]{1,0:T(8,128)(2,1)} %slice.156), channel_id=1, source_target_pairs={{0,1},{1,2},{2,3},{3,4},{4,5},{5,6},{6,7},{7,8},{8,9},{9,10},{10,1... | collective-permute-start | bytes 1572872 | tf_op jit(solution)/shard_map/ppermute | solution.py:16
  165.2 1.5 copy-start.13
  165.2 2.0 %copy-start.12 = (bf16[256,512]{0,1:T(8,128)(2,1)S(1)}, bf16[256,512]{0,1:T(8,128)(2,1)}, u32[]{:S(2)}) copy-start(bf16[256,512]{0,1:T(8,128)(2,1)} %copy.59) | copy-start | bytes 786436
  166.7 1.0 copy-start.11
  167.2 1.0 copy-start.10
  167.8 1.0 copy-start.9
  168.3 1.0 copy-start.8
  168.8 1.0 copy-start.7
  169.3 1.0 copy-start.6
  169.8 1.0 copy-start.5
  170.3 1.0 copy-start.4
  175.3 1.2 copy-start.24
  177.6 1.0 copy-start.21
  179.1 1.0 copy-start.19
  180.6 1.0 copy-start.17
  181.5 1.0 copy-start.16
  182.0 1.0 copy-start.15
  182.9 1.0 copy-start.14
  183.5 1.6 copy-start.2
  183.5 1.6 copy-start.3
  (5 other events, 4.8 us)
where the time goes:
time: 190 us; the launch traced here: 189 us
  local copies, waits for them, and re-layouts  69.8 us (37%)
  starting transfers between devices  46.9 us (25%)
  waiting for transfers between devices  46.3 us (24%)
  matrix products  16.9 us (9%)
  other arithmetic  7.18 us (4%)
    ppermute x9, waiting for transfers between devices, partner(): return lax.ppermute(value, axis, pairs)  46.3 us
    ppermute x9, starting transfers between devices, partner(): return lax.ppermute(value, axis, pairs)  41.3 us
    slice x23, local copies, waits for them, and re-layouts, attend_block(): value_heads = keyval[:, inner:].reshape(-1, head_count, head_size)  38.1 us
    slice x13, local copies, waits for them, and re-layouts, attend_block(): key_heads = keyval[:, :inner].reshape(-1, head_count, head_size)  22.4 us
    dot_general x12, matrix products, attend_block(): jnp.einsum('qhd,khd->hqk', query_heads, key_heads, preferred_element_type...  7.84 us
    dot_general x12, matrix products, attend_block(): jnp.einsum('hqk,khd->qhd', weights.astype(jnp.bfloat16), value_heads, pre...  6.93 us
    unnamed x74, local copies, waits for them, and re-layouts  5.2 us
    reduce_sum x12, other arithmetic, attend_block(): row_sum = jnp.sum(weights, axis=-1)  4.34 us
  transfers between devices with their start and end apart: 11, of which 2 were waited for; matrix products, arithmetic and copies ran while one was open for 31% of the time, Pallas kernels for 0%

commit v1 on v0

v1 whole, which is shorter than its diff:
```python
import functools
import math

import jax
import jax.numpy as jnp
from jax import lax
from jax.experimental import pallas as pl
from jax.experimental.pallas import tpu as pltpu
from jax.sharding import PartitionSpec as P

AXES = ("row", "col")
HEADS = 8
HD = 64
BLOCK = 256
INNER = HEADS * HD
WIDE = 3 * HD
SLOTS = 2
KEYS = 4
CHUNK = SLOTS * WIDE + 16
BACK = HD + 16
LOW = -1e30
SCALE = 1.0 / math.sqrt(HD)
LOG2E = math.log2(math.e)
Y_COUNT = 8
CORE_BIT = 4
VMEM_LIMIT = 32 * 1024 * 1024


def fields(index):
    return index & 7, (index >> 3) & 1, (index >> 4) & 1, (index >> 5) & 1, index >> 6


def split_groups(count):
    groups = {}
    for index in range(count):
        y, x_lo, core, x_hi, z = fields(index)
        key = (0, z, x_hi, x_lo) if core == 0 else (1, y, x_hi, x_lo)
        groups.setdefault(key, []).append(index)
    return [groups[key] for key in sorted(groups)]


def xor_pairs(count, bit):
    return [(index, index ^ (1 << bit)) for index in range(count)]


def edge_pairs(count):
    pairs = []
    for index in range(count):
        y = index % Y_COUNT
        if y == Y_COUNT - 1 and index + 1 < count:
            pairs.append((index, index + 1))
        if y == 0 and index > 0:
            pairs.append((index, index - 1))
    return pairs


def normalize(tokens, gain, shift):
    values = tokens.astype(jnp.float32)
    centred = values - jnp.mean(values, axis=-1, keepdims=True)
    row_var = jnp.mean(centred * centred, axis=-1, keepdims=True)
    return (centred * lax.rsqrt(row_var + 1e-05) * gain + shift).astype(jnp.bfloat16)


def key_times(index, links, core):
    y = index & 7
    bits = [(links >> bit) & 1 for bit in range(9)]
    odd = y & 1
    before = jnp.where(y > 0, 1 + odd * bits[0], 0)
    after = jnp.where(y < Y_COUNT - 1, 1 + (1 - odd) * bits[0], 0)
    along_y = (before, after, bits[1], bits[2])
    along_z = (jnp.int32(1), bits[6], bits[7], bits[8])
    return [jnp.where(core == 0, one, two) for one, two in zip(along_y, along_z)]


def key_members(member, core):
    along_y = (jnp.maximum(member - 1, 0), jnp.minimum(member + 1, HEADS - 1), member ^ 2, member ^ 4)
    along_z = (member, member ^ 1, member ^ 2, member ^ 4)
    return [jnp.where(core == 0, one, two) for one, two in zip(along_y, along_z)]


def stack_rows(rows, width, kind=jnp.float32):
    line = lax.broadcasted_iota(jnp.int32, (16, width), 0)
    table = jnp.zeros((16, width), kind)
    for entry, row in enumerate(rows):
        table = jnp.where(line == entry, row, table)
    return table


def norm_kernel(index_ref, links_ref, tokens_hbm, gain_hbm, shift_hbm, out_ref, tokens_ref, gain_ref, shift_ref, sems):
    copies = [
        pltpu.make_async_copy(source, target, sems.at[at])
        for at, (source, target) in enumerate(
            ((tokens_hbm, tokens_ref), (gain_hbm, gain_ref), (shift_hbm, shift_ref))
        )
    ]
    for copy in copies:
        copy.start()
    index = index_ref[0]
    times = key_times(index, links_ref[0], 1 - ((index >> CORE_BIT) & 1))
    out_ref[BLOCK:, :] = stack_rows(times, out_ref.shape[1], jnp.int32).astype(jnp.float32).astype(jnp.bfloat16)
    for copy in copies:
        copy.wait()
    out_ref[:BLOCK, :] = normalize(tokens_ref[...], gain_ref[...], shift_ref[...])


def project_kernel(index_ref, links_ref, own_ref, other_ref, w_hbm, chunk_ref, keyval_ref, normed_ref, w_ref, sems):
    tile = 4 * HD
    parts = 3 * INNER // tile
    copies = []
    for part in range(parts):
        columns = pl.ds(part * tile, tile)
        copies.append(pltpu.make_async_copy(w_hbm.at[:, columns], w_ref.at[:, columns], sems.at[part]))
        copies[-1].start()
    index = index_ref[0]
    times = key_times(index, links_ref[0], (index >> CORE_BIT) & 1)
    table = stack_rows(times, BLOCK, jnp.int32).astype(jnp.float32)
    sent = other_ref[BLOCK:, :BLOCK].astype(jnp.float32)
    line = lax.broadcasted_iota(jnp.int32, (16, BLOCK), 0)
    for entry in range(KEYS):
        table = jnp.where(line == KEYS + entry, sent[entry : entry + 1], table)
    for head in range(HEADS):
        chunk_ref[head, SLOTS * WIDE :, :] = table.astype(jnp.bfloat16)
    normed_ref[:BLOCK] = own_ref[:BLOCK]
    normed_ref[BLOCK:] = other_ref[:BLOCK]
    for part in range(parts):
        copies[part].wait()
        product = jnp.dot(
            normed_ref[...], w_ref[:, part * tile : (part + 1) * tile], preferred_element_type=jnp.float32
        )
        turned = product.T.astype(jnp.bfloat16)
        kind = part * tile // INNER
        for local in range(4):
            head = (part * tile % INNER) // HD + local
            rows = turned[local * HD : (local + 1) * HD]
            for slot in range(SLOTS):
                start = slot * WIDE + kind * HD
                chunk_ref[head, start : start + HD, :] = rows[:, slot * BLOCK : (slot + 1) * BLOCK]
            if kind > 0:
                keyval_ref[head, (kind - 1) * HD : kind * HD, :] = rows[:, :BLOCK]


def attend_all(items, score_ref, weight_ref):
    for at, (query, key, _) in enumerate(items):
        score_ref[at] = lax.dot_general(key(), query(), (((0,), (0,)), ((), ())), preferred_element_type=jnp.float32)
    stats = []
    for at in range(len(items)):
        scores = score_ref[at]
        peak = jnp.max(scores, axis=0, keepdims=True)
        weights = jnp.exp2((scores - peak) * (SCALE * LOG2E))
        stats.append((peak * SCALE, jnp.sum(weights, axis=0, keepdims=True)))
        weight_ref[at] = weights.astype(jnp.bfloat16)
    return [
        (jnp.dot(value(), weight_ref[at], preferred_element_type=jnp.float32),) + stats[at]
        for at, (_, _, value) in enumerate(items)
    ]


def merge(items):
    maxima = [jnp.where(times > 0, peak, LOW) for _, peak, _, times in items]
    top = functools.reduce(jnp.maximum, maxima)
    accum = total = None
    for (value, _, row_sum, times), peak in zip(items, maxima):
        factor = times * jnp.exp2((peak - top) * LOG2E)
        value, row_sum = factor * value.astype(jnp.bfloat16).astype(jnp.float32), factor * row_sum
        accum = value if accum is None else accum + value
        total = row_sum if total is None else total + row_sum
    return accum, top, total


def thirds(value):
    high = value.astype(jnp.bfloat16).astype(jnp.float32)
    rest = value - high
    middle = rest.astype(jnp.bfloat16).astype(jnp.float32)
    return [high, middle, rest - middle]


def group_kernel(index_ref, held_ref, back_ref, score_ref, weight_ref):
    core = (index_ref[0] >> CORE_BIT) & 1

    def step(member, carry):
        table = held_ref[member, SLOTS * WIDE :, :].astype(jnp.float32)
        sources = key_members(member, core)
        load = lambda source, start: lambda: held_ref[source, start : start + HD, :]
        items = [
            (load(member, slot * WIDE), load(source, slot * WIDE + HD), load(source, slot * WIDE + 2 * HD))
            for slot in range(SLOTS)
            for source in sources
        ]
        results = attend_all(items, score_ref, weight_ref)
        for slot in range(SLOTS):
            at = slot * KEYS
            accum, top, total = merge(
                [results[at + entry] + (table[at + entry : at + entry + 1],) for entry in range(KEYS)]
            )
            start = slot * BACK
            back_ref[member, start : start + HD, :] = accum.astype(jnp.bfloat16)
            back_ref[member, start + HD : start + BACK, :] = stack_rows(thirds(top) + thirds(total), BLOCK).astype(
                jnp.bfloat16
            )
        return carry

    lax.fori_loop(0, HEADS, step, 0)


def home_kernel(index_ref, links_ref, chunk_ref, x_lo_ref, x_hi_ref, edge_ref, out_ref, score_ref, weight_ref, count):
    index = index_ref[0]
    y = index & 7
    outer = ((y == 0) & (index > 0)) | ((y == Y_COUNT - 1) & (index < count - 1))
    times = [(links_ref[0] >> bit) & 1 for bit in (4, 3, 5)] + [jnp.where(outer, 1, 0)]
    rows = [jnp.full((1, BLOCK), number, jnp.int32).astype(jnp.float32) for number in times]

    def step(pair, carry):
        items = []
        load = lambda ref, head, start: lambda: ref[head, start : start + HD, :]
        for head in (2 * pair, 2 * pair + 1):
            query = load(chunk_ref, head, 0)
            items.append((query, load(chunk_ref, head, WIDE + HD), load(chunk_ref, head, WIDE + 2 * HD)))
            for ref in (x_lo_ref, x_hi_ref, edge_ref):
                items.append((query, load(ref, head, 0), load(ref, head, HD)))
        results = attend_all(items, score_ref, weight_ref)
        for local in range(2):
            accum, top, total = merge([results[local * KEYS + entry] + (rows[entry],) for entry in range(KEYS)])
            head = 2 * pair + local
            out_ref[head, :HD, :] = accum
            out_ref[head, HD:, :] = stack_rows([top, total], BLOCK)[:8]
        return carry

    lax.fori_loop(0, HEADS // 2, step, 0)


def finish_kernel(home_ref, own_ref, other_ref, out_ref):
    for pair in range(HEADS // 2):
        turned = []
        for head in (2 * pair, 2 * pair + 1):
            parts = [(home_ref[head, :HD, :], home_ref[head, HD : HD + 1, :], home_ref[head, HD + 1 : HD + 2, :])]
            for ref, slot in ((own_ref, 0), (other_ref, 1)):
                base = slot * BACK
                value = ref[head, base : base + HD, :].astype(jnp.float32)
                stats = ref[head, base + HD : base + BACK, :].astype(jnp.float32)
                parts.append((value, stats[0:1] + stats[1:2] + stats[2:3], stats[3:4] + stats[4:5] + stats[5:6]))
            top = functools.reduce(jnp.maximum, [peak for _, peak, _ in parts])
            factors = [jnp.exp2((peak - top) * LOG2E) for _, peak, _ in parts]
            accum = sum(factor * value for factor, (value, _, _) in zip(factors, parts))
            total = sum(factor * row_sum for factor, (_, _, row_sum) in zip(factors, parts))
            turned.append(accum / total)
        out_ref[:, pair * 2 * HD : (pair + 1) * 2 * HD] = jnp.concatenate(turned, axis=0).T


SMEM = pl.BlockSpec(memory_space=pltpu.SMEM)
WHOLE = pl.BlockSpec(memory_space=pltpu.VMEM)
HBM = pl.BlockSpec(memory_space=pltpu.HBM)


def call(kernel, specs, shapes, scratch, flops, moved, *operands):
    return pl.pallas_call(
        kernel,
        in_specs=specs,
        out_specs=[WHOLE] * len(shapes) if isinstance(shapes, list) else WHOLE,
        out_shape=shapes,
        scratch_shapes=scratch,
        compiler_params=pltpu.CompilerParams(vmem_limit_bytes=VMEM_LIMIT),
        cost_estimate=pl.CostEstimate(flops=flops, bytes_accessed=moved, transcendentals=0),
    )(*operands)


def per_device(tokens, norm_gain, norm_shift, w_qkv, links, count):
    groups = split_groups(count)
    width = w_qkv.shape[0]
    bf16, f32 = jnp.bfloat16, jnp.float32
    index = (lax.axis_index("row") * lax.axis_size("col") + lax.axis_index("col")).astype(jnp.int32)[None]
    attend_scratch = [pltpu.VMEM((2 * KEYS, BLOCK, BLOCK), f32), pltpu.VMEM((2 * KEYS, BLOCK, BLOCK), bf16)]
    normed = call(
        norm_kernel,
        [SMEM] * 2 + [HBM] * 3,
        jax.ShapeDtypeStruct((BLOCK + 16, width), bf16),
        [
            pltpu.VMEM((BLOCK, width), bf16),
            pltpu.VMEM((1, width), f32),
            pltpu.VMEM((1, width), f32),
            pltpu.SemaphoreType.DMA((3,)),
        ],
        10**7,
        2**20,
        index,
        links,
        tokens,
        norm_gain[None, :],
        norm_shift[None, :],
    )
    other = lax.ppermute(normed, AXES, xor_pairs(count, CORE_BIT))
    chunks, keyval = call(
        project_kernel,
        [SMEM] * 2 + [WHOLE] * 2 + [HBM],
        [jax.ShapeDtypeStruct((HEADS, CHUNK, BLOCK), bf16), jax.ShapeDtypeStruct((HEADS, 2 * HD, BLOCK), bf16)],
        [pltpu.VMEM((2 * BLOCK, width), bf16), pltpu.VMEM(w_qkv.shape, bf16), pltpu.SemaphoreType.DMA((6,))],
        2 * 2 * BLOCK * w_qkv.shape[0] * w_qkv.shape[1],
        6 * 2**20,
        index,
        links,
        normed,
        other,
        w_qkv,
    )
    held = lax.all_to_all(chunks, AXES, 0, 0, axis_index_groups=groups, tiled=True)
    from_x_lo = lax.ppermute(keyval, AXES, xor_pairs(count, 3))
    from_x_hi = lax.ppermute(keyval, AXES, xor_pairs(count, 5))
    back = call(
        group_kernel,
        [SMEM, WHOLE],
        jax.ShapeDtypeStruct((HEADS, SLOTS * BACK, BLOCK), bf16),
        attend_scratch,
        64 * 4 * BLOCK * BLOCK * 256,
        3 * 2**20,
        index,
        held,
    )
    keyval, held = lax.optimization_barrier((keyval, held))
    from_edge = lax.ppermute(keyval, AXES, edge_pairs(count))
    back, from_x_lo, from_x_hi = lax.optimization_barrier((back, from_x_lo, from_x_hi))
    mine = lax.all_to_all(back, AXES, 0, 0, axis_index_groups=groups, tiled=True)
    home = call(
        functools.partial(home_kernel, count=count),
        [SMEM] * 2 + [WHOLE] * 4,
        jax.ShapeDtypeStruct((HEADS, HD + 8, BLOCK), f32),
        attend_scratch,
        32 * 4 * BLOCK * BLOCK * 256,
        4 * 2**20,
        index,
        links,
        chunks,
        from_x_lo,
        from_x_hi,
        from_edge,
    )
    theirs = lax.ppermute(mine, AXES, xor_pairs(count, CORE_BIT))
    return call(
        finish_kernel,
        [WHOLE] * 3,
        jax.ShapeDtypeStruct((BLOCK, INNER), f32),
        [],
        10**7,
        2 * 2**20,
        home,
        mine,
        theirs,
    )


def solution(mesh):
    placed = (P(AXES, None), P(), P(), P(), P(AXES))
    return jax.shard_map(
        functools.partial(per_device, count=mesh.size),
        mesh=mesh,
        in_specs=placed,
        out_specs=P(AXES, None),
        check_vma=False,
    )
```

time: 190 us -> 92.1 us (0.48)
  local copies, waits for them, and re-layouts: 69.8 us -> 4.3 us
  Pallas kernels: 0 us -> 21.8 us
  matrix products: 16.9 us -> 0 us
  starting transfers between devices: 46.9 us -> 31.6 us
  waiting for transfers between devices: 46.3 us -> 33.1 us
  other arithmetic: 7.18 us -> 0 us
    slice x38 -> x0, local copies, waits for them, and re-layouts: 62.4 us -> none  [the longest x23 38.1 us: attend_block(): value_heads = keyval[:, inner:].reshape(-1, head_count, head_size)]
    ppermute x11 -> x5, waiting for transfers between devices: 46.3 us -> 6.7 us  [the longest x1 5.13 us: per_device(): from_edge = lax.ppermute(keyval, AXES, edge_pairs(count))]
    all_to_all x0 -> x2, waiting for transfers between devices: none -> 26.4 us  [the longest x1 16.7 us: per_device(): lax.all_to_all(chunks, AXES, 0, 0, axis_index_groups=groups, tiled=True)]
    ppermute x11 -> x5, starting transfers between devices: 46.9 us -> 23.4 us  [the longest x1 8.79 us: per_device(): other = lax.ppermute(normed, AXES, xor_pairs(count, CORE_BIT))]
    pallas_call x0 -> x5, Pallas kernels: none -> 21.8 us  [call(): pl.pallas_call(kernel, in_specs=specs, out_specs=[WHOLE] * len(shapes) if...]
    dot_general x25 -> x0, matrix products: 16.9 us -> none  [the longest x12 7.84 us: attend_block(): jnp.einsum('qhd,khd->hqk', query_heads, key_heads, preferred_element_type...]
    all_to_all x0 -> x2, starting transfers between devices: none -> 8.22 us  [the longest x1 4.67 us: per_device(): lax.all_to_all(chunks, AXES, 0, 0, axis_index_groups=groups, tiled=True)]
    reduce_sum x15 -> x0, other arithmetic: 7.09 us -> none  [the longest x12 4.34 us: attend_block(): row_sum = jnp.sum(weights, axis=-1)]
  transfers between devices with their start and end apart: 11 -> 7, of which waited for: 2 -> 4; matrix products, arithmetic and copies ran while one was open for 31% -> 0% of each run, Pallas kernels for 0% -> 15%
where the time goes in v1:
time: 92.1 us; the launch traced here: 91.5 us
  waiting for transfers between devices  33.1 us (36%)
  starting transfers between devices  31.6 us (34%)
  Pallas kernels  21.8 us (24%)
  local copies, waits for them, and re-layouts  4.3 us (5%)
    pallas_call x5, Pallas kernels, call(): pl.pallas_call(kernel, in_specs=specs, out_specs=[WHOLE] * len(shapes) if...  21.8 us
    all_to_all x1, waiting for transfers between devices, per_device(): lax.all_to_all(chunks, AXES, 0, 0, axis_index_groups=groups, tiled=True)  16.7 us
    all_to_all x1, waiting for transfers between devices, per_device(): lax.all_to_all(back, AXES, 0, 0, axis_index_groups=groups, tiled=True)  9.65 us
    ppermute x1, starting transfers between devices, per_device(): other = lax.ppermute(normed, AXES, xor_pairs(count, CORE_BIT))  8.79 us
    ppermute x1, waiting for transfers between devices, per_device(): from_edge = lax.ppermute(keyval, AXES, edge_pairs(count))  5.13 us
    all_to_all x1, starting transfers between devices, per_device(): lax.all_to_all(chunks, AXES, 0, 0, axis_index_groups=groups, tiled=True)  4.67 us
    ppermute x1, starting transfers between devices, per_device(): from_x_hi = lax.ppermute(keyval, AXES, xor_pairs(count, 5))  4.36 us
    unnamed x8, local copies, waits for them, and re-layouts  4.3 us
  transfers between devices with their start and end apart: 7, of which 4 were waited for; matrix products, arithmetic and copies ran while one was open for 0% of the time, Pallas kernels for 15%

profile of v1, /device:TPU:1, one launch (start us, length us, event | category | flops | bytes accessed | tf_op | source)
XLA Modules:
  0.0 91.5 jit_solution(15503482933917160203)
XLA Ops:
  0.7 0.0 copy-start
  0.7 1.0 %copy-done = bf16[256,1024]{1,0:T(8,128)(2,1)S(1)} copy-done((bf16[256,1024]{1,0:T(8,128)(2,1)S(1)}, bf16[256,1024]{1,0:T(8,128)(2,1)}, u32[]{:S(2)}) %copy-start) | copy-done | bytes 524312
  1.7 0.0 copy-start.1
  1.7 0.7 copy-done.1
  2.4 0.0 copy-start.2
  2.4 0.7 copy-done.2
  3.1 0.5 shard_map.55.own_ref
  3.5 8.8 %collective-permute-start = (bf16[272,1024]{1,0:T(8,128)(2,1)S(1)}, bf16[272,1024]{1,0:T(8,128)(2,1)S(1)}, u32[]{:S(2)}, u32[]{:S(2)}) collective-permute-start(bf16[272,1024]{1,0:T(8,128)(2,1)S(1)} %shard_map.55.own_ref), channel_id=1, source_target_pairs={{0,16},{1,17},{2,18},{3,19},{4,20},{5,21},{6,22},{7,23},{8,24},{9,... | collective-permute-start | bytes 1671176 | tf_op jit(solution)/shard_map/ppermute | solution.py:290
  12.3 1.6 %collective-permute-done.other_ref = bf16[272,1024]{1,0:T(8,128)(2,1)S(1)} collective-permute-done((bf16[272,1024]{1,0:T(8,128)(2,1)S(1)}, bf16[272,1024]{1,0:T(8,128)(2,1)S(1)}, u32[]{:S(2)}, u32[]{:S(2)}) %collective-permute-start) | collective-permute-done | bytes 557088 | tf_op jit(solution)/shard_map/ppermute | solution.py:290
  13.9 0.0 copy-start.3
  13.9 1.9 %copy-done.3 = bf16[1024,1536]{1,0:T(8,128)(2,1)S(1)} copy-done((bf16[1024,1536]{1,0:T(8,128)(2,1)S(1)}, bf16[1024,1536]{1,0:T(8,128)(2,1)}, u32[]{:S(2)}) %copy-start.3) | copy-done | bytes 3145752
  15.8 6.1 %shard_map.56 = (bf16[8,400,256]{2,1,0:T(8,128)(2,1)}, bf16[8,128,256]{2,1,0:T(8,128)(2,1)S(1)}) custom-call(s32[1]{0:T(128)} %bitcast.index_ref, s32[1]{0:T(128)S(6)} %copy.6.links_ref, bf16[272,1024]{1,0:T(8,128)(2,1)S(1)} %shard_map.55.own_ref, bf16[272,1024]{1,0:T(8,128)(2,1)S(1)} %collective-permute-done.other_ref, bf16[1024,1536]{1,0:T(8,128)(2,1)S(1)} %copy-done.3), custom_call_target="tpu_custom_call" | custom-call | flops 1610612736 | bytes 6291456 | tf_op jit(solution)/shard_map/pallas_call | solution.py:255
  21.9 4.7 %all-to-all-start = ((bf16[8,400,256]{2,1,0:T(8,128)(2,1)}), bf16[8,400,256]{2,1,0:T(8,128)(2,1)S(1)}, u32[]{:S(2)}, u32[]{:S(2)}) async-start(bf16[8,400,256]{2,1,0:T(8,128)(2,1)} %get-tuple-element.11.chunk_ref), calls=%async_computation | async-start | bytes 3276800 | tf_op jit(solution)/shard_map/all_to_all | solution.py:304
  26.6 3.1 %collective-permute-start.1 = (bf16[8,128,256]{2,1,0:T(8,128)(2,1)S(1)}, bf16[8,128,256]{2,1,0:T(8,128)(2,1)S(1)}, u32[]{:S(2)}, u32[]{:S(2)}) collective-permute-start(bf16[8,128,256]{2,1,0:T(8,128)(2,1)S(1)} %get-tuple-element.15), channel_id=1, source_target_pairs={{0,8},{1,9},{2,10},{3,11},{4,12},{5,13},{6,14},{7,15},{8,0},{9,1},... | collective-permute-start | bytes 1572872 | tf_op jit(solution)/shard_map/ppermute | solution.py:305
  29.7 4.4 %collective-permute-start.2 = (bf16[8,128,256]{2,1,0:T(8,128)(2,1)S(1)}, bf16[8,128,256]{2,1,0:T(8,128)(2,1)S(1)}, u32[]{:S(2)}, u32[]{:S(2)}) collective-permute-start(bf16[8,128,256]{2,1,0:T(8,128)(2,1)S(1)} %get-tuple-element.15), channel_id=1, source_target_pairs={{0,32},{1,33},{2,34},{3,35},{4,36},{5,37},{6,38},{7,39},{8,40},{9,... | collective-permute-start | bytes 1572872 | tf_op jit(solution)/shard_map/ppermute | solution.py:306
  34.0 16.7 %all-to-all-done.held_ref = bf16[8,400,256]{2,1,0:T(8,128)(2,1)S(1)} async-done(((bf16[8,400,256]{2,1,0:T(8,128)(2,1)}), bf16[8,400,256]{2,1,0:T(8,128)(2,1)S(1)}, u32[]{:S(2)}, u32[]{:S(2)}) %all-to-all-start) | async-done | bytes 1638432 | tf_op jit(solution)/shard_map/all_to_all | solution.py:304
  50.8 8.9 %shard_map.57 = bf16[8,160,256]{2,1,0:T(8,128)(2,1)} custom-call(s32[1]{0:T(128)} %bitcast.index_ref, bf16[8,400,256]{2,1,0:T(8,128)(2,1)S(1)} %all-to-all-done.held_ref), custom_call_target="tpu_custom_call" | custom-call | flops 4294967296 | bytes 3145728 | tf_op jit(solution)/shard_map/pallas_call | solution.py:255
  59.6 0.0 collective-permute-done.1.x_lo_ref
  59.6 0.0 collective-permute-done.2.x_hi_ref
  59.6 3.5 %all-to-all-start.1 = ((bf16[8,160,256]{2,1,0:T(8,128)(2,1)}), bf16[8,160,256]{2,1,0:T(8,128)(2,1)S(1)}, u32[]{:S(2)}, u32[]{:S(2)}) async-start(bf16[8,160,256]{2,1,0:T(8,128)(2,1)} %shard_map.57), calls=%async_computation.1 | async-start | bytes 1310720 | tf_op jit(solution)/shard_map/all_to_all | solution.py:320
  63.2 4.1 %collective-permute-start.3 = (bf16[8,128,256]{2,1,0:T(8,128)(2,1)S(1)}, bf16[8,128,256]{2,1,0:T(8,128)(2,1)S(1)}, u32[]{:S(2)}, u32[]{:S(2)}) collective-permute-start(bf16[8,128,256]{2,1,0:T(8,128)(2,1)S(1)} %get-tuple-element.15), channel_id=1, source_target_pairs={{7,8},{8,7},{15,16},{16,15},{23,24},{24,23},{31,32},{32,31},{39,40... | collective-permute-start | bytes 1572872 | tf_op jit(solution)/shard_map/ppermute | solution.py:318
  67.3 9.7 %all-to-all-done.1.own_ref = bf16[8,160,256]{2,1,0:T(8,128)(2,1)S(1)} async-done(((bf16[8,160,256]{2,1,0:T(8,128)(2,1)}), bf16[8,160,256]{2,1,0:T(8,128)(2,1)S(1)}, u32[]{:S(2)}, u32[]{:S(2)}) %all-to-all-start.1) | async-done | bytes 655392 | tf_op jit(solution)/shard_map/all_to_all | solution.py:320
  77.0 3.0 %collective-permute-start.4 = (bf16[8,160,256]{2,1,0:T(8,128)(2,1)S(1)}, bf16[8,160,256]{2,1,0:T(8,128)(2,1)S(1)}, u32[]{:S(2)}, u32[]{:S(2)}) collective-permute-start(bf16[8,160,256]{2,1,0:T(8,128)(2,1)S(1)} %all-to-all-done.1.own_ref), channel_id=1, source_target_pairs={{0,16},{1,17},{2,18},{3,19},{4,20},{5,21},{6,22},{7,23},{8,24},{9,... | collective-permute-start | bytes 1966088 | tf_op jit(solution)/shard_map/ppermute | solution.py:335
  80.0 5.1 %collective-permute-done.3.edge_ref = bf16[8,128,256]{2,1,0:T(8,128)(2,1)S(1)} collective-permute-done((bf16[8,128,256]{2,1,0:T(8,128)(2,1)S(1)}, bf16[8,128,256]{2,1,0:T(8,128)(2,1)S(1)}, u32[]{:S(2)}, u32[]{:S(2)}) %collective-permute-start.3) | collective-permute-done | bytes 524320 | tf_op jit(solution)/shard_map/ppermute | solution.py:318
  85.1 5.3 %shard_map.58.home_ref = f32[8,72,256]{2,1,0:T(8,128)S(1)} custom-call(s32[1]{0:T(128)} %bitcast.index_ref, s32[1]{0:T(128)S(6)} %copy.6.links_ref, bf16[8,400,256]{2,1,0:T(8,128)(2,1)} %get-tuple-element.11.chunk_ref, bf16[8,128,256]{2,1,0:T(8,128)(2,1)S(1)} %collective-permute-done.1.x_lo_ref, bf16[8,128,256]{2,1,0:T(8,128)(2,1)S(1)} %collective-permute-done.2.x_hi_ref, ...), custom_call_target="tpu_custom_call" | custom-call | flops 2147483648 | bytes 4194304 | tf_op jit(solution)/shard_map/pallas_call | solution.py:255
  90.4 0.0 collective-permute-done.4.other_ref
  90.5 1.1 %shard_map.59 = f32[256,512]{1,0:T(8,128)} custom-call(f32[8,72,256]{2,1,0:T(8,128)S(1)} %shard_map.58.home_ref, bf16[8,160,256]{2,1,0:T(8,128)(2,1)S(1)} %all-to-all-done.1.own_ref, bf16[8,160,256]{2,1,0:T(8,128)(2,1)S(1)} %collective-permute-done.4.other_ref), custom_call_target="tpu_custom_call" | custom-call | flops 10000000 | bytes 2097152 | tf_op jit(solution)/shard_map/pallas_call | solution.py:255
Async XLA Ops:
  0.7 1.0 %copy-start = (bf16[256,1024]{1,0:T(8,128)(2,1)S(1)}, bf16[256,1024]{1,0:T(8,128)(2,1)}, u32[]{:S(2)}) copy-start(bf16[256,1024]{1,0:T(8,128)(2,1)} %tokens_hbm.1) | copy-start | bytes 1572868
  1.7 0.7 copy-start.1
  2.4 0.7 copy-start.2
  3.5 10.4 %collective-permute-start = (bf16[272,1024]{1,0:T(8,128)(2,1)S(1)}, bf16[272,1024]{1,0:T(8,128)(2,1)S(1)}, u32[]{:S(2)}, u32[]{:S(2)}) collective-permute-start(bf16[272,1024]{1,0:T(8,128)(2,1)S(1)} %shard_map.55.own_ref), channel_id=1, source_target_pairs={{0,16},{1,17},{2,18},{3,19},{4,20},{5,21},{6,22},{7,23},{8,24},{9,... | collective-permute-start | bytes 1671176 | tf_op jit(solution)/shard_map/ppermute | solution.py:290
  13.9 1.9 %copy-start.3 = (bf16[1024,1536]{1,0:T(8,128)(2,1)S(1)}, bf16[1024,1536]{1,0:T(8,128)(2,1)}, u32[]{:S(2)}) copy-start(bf16[1024,1536]{1,0:T(8,128)(2,1)} %w_hbm.1) | copy-start | bytes 9437188
  21.9 28.9 %all-to-all-start = ((bf16[8,400,256]{2,1,0:T(8,128)(2,1)}), bf16[8,400,256]{2,1,0:T(8,128)(2,1)S(1)}, u32[]{:S(2)}, u32[]{:S(2)}) async-start(bf16[8,400,256]{2,1,0:T(8,128)(2,1)} %get-tuple-element.11.chunk_ref), calls=%async_computation | async-start | bytes 3276800 | tf_op jit(solution)/shard_map/all_to_all | solution.py:304
  26.6 33.1 %collective-permute-start.1 = (bf16[8,128,256]{2,1,0:T(8,128)(2,1)S(1)}, bf16[8,128,256]{2,1,0:T(8,128)(2,1)S(1)}, u32[]{:S(2)}, u32[]{:S(2)}) collective-permute-start(bf16[8,128,256]{2,1,0:T(8,128)(2,1)S(1)} %get-tuple-element.15), channel_id=1, source_target_pairs={{0,8},{1,9},{2,10},{3,11},{4,12},{5,13},{6,14},{7,15},{8,0},{9,1},... | collective-permute-start | bytes 1572872 | tf_op jit(solution)/shard_map/ppermute | solution.py:305
  29.7 30.0 %collective-permute-start.2 = (bf16[8,128,256]{2,1,0:T(8,128)(2,1)S(1)}, bf16[8,128,256]{2,1,0:T(8,128)(2,1)S(1)}, u32[]{:S(2)}, u32[]{:S(2)}) collective-permute-start(bf16[8,128,256]{2,1,0:T(8,128)(2,1)S(1)} %get-tuple-element.15), channel_id=1, source_target_pairs={{0,32},{1,33},{2,34},{3,35},{4,36},{5,37},{6,38},{7,39},{8,40},{9,... | collective-permute-start | bytes 1572872 | tf_op jit(solution)/shard_map/ppermute | solution.py:306
  59.6 17.4 %all-to-all-start.1 = ((bf16[8,160,256]{2,1,0:T(8,128)(2,1)}), bf16[8,160,256]{2,1,0:T(8,128)(2,1)S(1)}, u32[]{:S(2)}, u32[]{:S(2)}) async-start(bf16[8,160,256]{2,1,0:T(8,128)(2,1)} %shard_map.57), calls=%async_computation.1 | async-start | bytes 1310720 | tf_op jit(solution)/shard_map/all_to_all | solution.py:320
  63.2 22.0 %collective-permute-start.3 = (bf16[8,128,256]{2,1,0:T(8,128)(2,1)S(1)}, bf16[8,128,256]{2,1,0:T(8,128)(2,1)S(1)}, u32[]{:S(2)}, u32[]{:S(2)}) collective-permute-start(bf16[8,128,256]{2,1,0:T(8,128)(2,1)S(1)} %get-tuple-element.15), channel_id=1, source_target_pairs={{7,8},{8,7},{15,16},{16,15},{23,24},{24,23},{31,32},{32,31},{39,40... | collective-permute-start | bytes 1572872 | tf_op jit(solution)/shard_map/ppermute | solution.py:318
  77.0 13.5 %collective-permute-start.4 = (bf16[8,160,256]{2,1,0:T(8,128)(2,1)S(1)}, bf16[8,160,256]{2,1,0:T(8,128)(2,1)S(1)}, u32[]{:S(2)}, u32[]{:S(2)}) collective-permute-start(bf16[8,160,256]{2,1,0:T(8,128)(2,1)S(1)} %all-to-all-done.1.own_ref), channel_id=1, source_target_pairs={{0,16},{1,17},{2,18},{3,19},{4,20},{5,21},{6,22},{7,23},{8,24},{9,... | collective-permute-start | bytes 1966088 | tf_op jit(solution)/shard_map/ppermute | solution.py:335

commit v2 on v1

--- a/solution.py
+++ b/solution.py
@@ -16,14 +16,15 @@
 WIDE = 3 * HD
 SLOTS = 2
 KEYS = 4
-CHUNK = SLOTS * WIDE + 16
-BACK = HD + 16
+CHUNK = SLOTS * WIDE + 8
+BACK = SLOTS * HD + 8
 LOW = -1e30
 SCALE = 1.0 / math.sqrt(HD)
 LOG2E = math.log2(math.e)
 Y_COUNT = 8
 CORE_BIT = 4
 VMEM_LIMIT = 32 * 1024 * 1024
+WIDE_LIMIT = 56 * 1024 * 1024
 
 
 def fields(index):
@@ -78,9 +79,9 @@
     return [jnp.where(core == 0, one, two) for one, two in zip(along_y, along_z)]
 
 
-def stack_rows(rows, width, kind=jnp.float32):
-    line = lax.broadcasted_iota(jnp.int32, (16, width), 0)
-    table = jnp.zeros((16, width), kind)
+def stack_rows(rows, height, width, kind=jnp.float32):
+    line = lax.broadcasted_iota(jnp.int32, (height, width), 0)
+    table = jnp.zeros((height, width), kind)
     for entry, row in enumerate(rows):
         table = jnp.where(line == entry, row, table)
     return table
@@ -97,46 +98,51 @@
         copy.start()
     index = index_ref[0]
     times = key_times(index, links_ref[0], 1 - ((index >> CORE_BIT) & 1))
-    out_ref[BLOCK:, :] = stack_rows(times, out_ref.shape[1], jnp.int32).astype(jnp.float32).astype(jnp.bfloat16)
+    out_ref[BLOCK:, :] = stack_rows(times, 16, out_ref.shape[1], jnp.int32).astype(jnp.float32).astype(jnp.bfloat16)
     for copy in copies:
         copy.wait()
     out_ref[:BLOCK, :] = normalize(tokens_ref[...], gain_ref[...], shift_ref[...])
 
 
-def project_kernel(index_ref, links_ref, own_ref, other_ref, w_hbm, chunk_ref, keyval_ref, normed_ref, w_ref, sems):
+def project(normed_ref, w_ref, kinds, store):
     tile = 4 * HD
-    parts = 3 * INNER // tile
-    copies = []
-    for part in range(parts):
-        columns = pl.ds(part * tile, tile)
-        copies.append(pltpu.make_async_copy(w_hbm.at[:, columns], w_ref.at[:, columns], sems.at[part]))
-        copies[-1].start()
+    for kind in kinds:
+        for start in range(0, INNER, tile):
+            columns = w_ref[:, kind * INNER + start : kind * INNER + start + tile]
+            product = jnp.dot(normed_ref[...], columns, preferred_element_type=jnp.float32)
+            turned = product.T.astype(jnp.bfloat16)
+            for local in range(4):
+                store(kind, start // HD + local, turned[local * HD : (local + 1) * HD])
+
+
+def project_kernel(index_ref, links_ref, own_ref, other_ref, w_ref, chunk_ref, keyval_ref, normed_ref):
     index = index_ref[0]
     times = key_times(index, links_ref[0], (index >> CORE_BIT) & 1)
-    table = stack_rows(times, BLOCK, jnp.int32).astype(jnp.float32)
+    table = stack_rows(times, 8, BLOCK, jnp.int32).astype(jnp.float32)
     sent = other_ref[BLOCK:, :BLOCK].astype(jnp.float32)
-    line = lax.broadcasted_iota(jnp.int32, (16, BLOCK), 0)
+    line = lax.broadcasted_iota(jnp.int32, (8, BLOCK), 0)
     for entry in range(KEYS):
         table = jnp.where(line == KEYS + entry, sent[entry : entry + 1], table)
     for head in range(HEADS):
         chunk_ref[head, SLOTS * WIDE :, :] = table.astype(jnp.bfloat16)
     normed_ref[:BLOCK] = own_ref[:BLOCK]
     normed_ref[BLOCK:] = other_ref[:BLOCK]
-    for part in range(parts):
-        copies[part].wait()
-        product = jnp.dot(
-            normed_ref[...], w_ref[:, part * tile : (part + 1) * tile], preferred_element_type=jnp.float32
-        )
-        turned = product.T.astype(jnp.bfloat16)
-        kind = part * tile // INNER
-        for local in range(4):
-            head = (part * tile % INNER) // HD + local
-            rows = turned[local * HD : (local + 1) * HD]
-            for slot in range(SLOTS):
-                start = slot * WIDE + kind * HD
-                chunk_ref[head, start : start + HD, :] = rows[:, slot * BLOCK : (slot + 1) * BLOCK]
-            if kind > 0:
-                keyval_ref[head, (kind - 1) * HD : kind * HD, :] = rows[:, :BLOCK]
+
+    def store(kind, head, rows):
+        for slot in range(SLOTS):
+            start = slot * WIDE + kind * HD
+            chunk_ref[head, start : start + HD, :] = rows[:, slot * BLOCK : (slot + 1) * BLOCK]
+        if kind > 0:
+            keyval_ref[head, (kind - 1) * HD : kind * HD, :] = rows[:, :BLOCK]
+
+    project(normed_ref, w_ref, (0, 1, 2), store)
+
+
+def edge_kernel(normed_ref, w_ref, keyval_ref):
+    def store(kind, head, rows):
+        keyval_ref[head, (kind - 1) * HD : kind * HD, :] = rows
+
+    project(normed_ref.at[pl.ds(0, BLOCK)], w_ref, (1, 2), store)
 
 
 def attend_all(items, score_ref, weight_ref):
@@ -187,16 +193,15 @@
             for source in sources
         ]
         results = attend_all(items, score_ref, weight_ref)
+        stats = []
         for slot in range(SLOTS):
             at = slot * KEYS
             accum, top, total = merge(
                 [results[at + entry] + (table[at + entry : at + entry + 1],) for entry in range(KEYS)]
             )
-            start = slot * BACK
-            back_ref[member, start : start + HD, :] = accum.astype(jnp.bfloat16)
-            back_ref[member, start + HD : start + BACK, :] = stack_rows(thirds(top) + thirds(total), BLOCK).astype(
-                jnp.bfloat16
-            )
+            back_ref[member, slot * HD : (slot + 1) * HD, :] = (accum / total).astype(jnp.bfloat16)
+            stats.extend(thirds(top + jnp.log(total)))
+        back_ref[member, SLOTS * HD :, :] = stack_rows(stats, 8, BLOCK).astype(jnp.bfloat16)
         return carry
 
     lax.fori_loop(0, HEADS, step, 0)
@@ -222,7 +227,7 @@
             accum, top, total = merge([results[local * KEYS + entry] + (rows[entry],) for entry in range(KEYS)])
             head = 2 * pair + local
             out_ref[head, :HD, :] = accum
-            out_ref[head, HD:, :] = stack_rows([top, total], BLOCK)[:8]
+            out_ref[head, HD:, :] = stack_rows([top, total], 8, BLOCK)
         return carry
 
     lax.fori_loop(0, HEADS // 2, step, 0)
@@ -232,12 +237,13 @@
     for pair in range(HEADS // 2):
         turned = []
         for head in (2 * pair, 2 * pair + 1):
-            parts = [(home_ref[head, :HD, :], home_ref[head, HD : HD + 1, :], home_ref[head, HD + 1 : HD + 2, :])]
+            home_top = home_ref[head, HD : HD + 1, :]
+            parts = [(home_ref[head, :HD, :], home_top, home_ref[head, HD + 1 : HD + 2, :])]
             for ref, slot in ((own_ref, 0), (other_ref, 1)):
-                base = slot * BACK
-                value = ref[head, base : base + HD, :].astype(jnp.float32)
-                stats = ref[head, base + HD : base + BACK, :].astype(jnp.float32)
-                parts.append((value, stats[0:1] + stats[1:2] + stats[2:3], stats[3:4] + stats[4:5] + stats[5:6]))
+                value = ref[head, slot * HD : (slot + 1) * HD, :].astype(jnp.float32)
+                stats = ref[head, SLOTS * HD :, :].astype(jnp.float32)
+                at = 3 * slot
+                parts.append((value, stats[at : at + 1] + stats[at + 1 : at + 2] + stats[at + 2 : at + 3], 1.0))
             top = functools.reduce(jnp.maximum, [peak for _, peak, _ in parts])
             factors = [jnp.exp2((peak - top) * LOG2E) for _, peak, _ in parts]
             accum = sum(factor * value for factor, (value, _, _) in zip(factors, parts))
@@ -251,14 +257,14 @@
 HBM = pl.BlockSpec(memory_space=pltpu.HBM)
 
 
-def call(kernel, specs, shapes, scratch, flops, moved, *operands):
+def call(kernel, specs, shapes, scratch, flops, moved, *operands, limit=VMEM_LIMIT):
     return pl.pallas_call(
         kernel,
         in_specs=specs,
         out_specs=[WHOLE] * len(shapes) if isinstance(shapes, list) else WHOLE,
         out_shape=shapes,
         scratch_shapes=scratch,
-        compiler_params=pltpu.CompilerParams(vmem_limit_bytes=VMEM_LIMIT),
+        compiler_params=pltpu.CompilerParams(vmem_limit_bytes=limit),
         cost_estimate=pl.CostEstimate(flops=flops, bytes_accessed=moved, transcendentals=0),
     )(*operands)
 
@@ -279,21 +285,23 @@
             pltpu.VMEM((1, width), f32),
             pltpu.SemaphoreType.DMA((3,)),
         ],
-        10**7,
+        13 * 10**9,
         2**20,
         index,
         links,
         tokens,
         norm_gain[None, :],
         norm_shift[None, :],
+        limit=WIDE_LIMIT,
     )
     other = lax.ppermute(normed, AXES, xor_pairs(count, CORE_BIT))
+    edge = lax.ppermute(normed, AXES, edge_pairs(count))
     chunks, keyval = call(
         project_kernel,
-        [SMEM] * 2 + [WHOLE] * 2 + [HBM],
+        [SMEM] * 2 + [WHOLE] * 3,
         [jax.ShapeDtypeStruct((HEADS, CHUNK, BLOCK), bf16), jax.ShapeDtypeStruct((HEADS, 2 * HD, BLOCK), bf16)],
-        [pltpu.VMEM((2 * BLOCK, width), bf16), pltpu.VMEM(w_qkv.shape, bf16), pltpu.SemaphoreType.DMA((6,))],
-        2 * 2 * BLOCK * w_qkv.shape[0] * w_qkv.shape[1],
+        [pltpu.VMEM((2 * BLOCK, width), bf16)],
+        20 * 2 * 2 * BLOCK * w_qkv.shape[0] * w_qkv.shape[1],
         6 * 2**20,
         index,
         links,
@@ -302,28 +310,37 @@
         w_qkv,
     )
     held = lax.all_to_all(chunks, AXES, 0, 0, axis_index_groups=groups, tiled=True)
+    from_edge = call(
+        edge_kernel,
+        [WHOLE] * 2,
+        jax.ShapeDtypeStruct((HEADS, 2 * HD, BLOCK), bf16),
+        [],
+        40 * 2 * BLOCK * w_qkv.shape[0] * w_qkv.shape[1],
+        4 * 2**20,
+        edge,
+        w_qkv,
+    )
+    keyval, from_edge = lax.optimization_barrier((keyval, from_edge))
     from_x_lo = lax.ppermute(keyval, AXES, xor_pairs(count, 3))
     from_x_hi = lax.ppermute(keyval, AXES, xor_pairs(count, 5))
+    held, from_edge = lax.optimization_barrier((held, from_edge))
     back = call(
         group_kernel,
         [SMEM, WHOLE],
-        jax.ShapeDtypeStruct((HEADS, SLOTS * BACK, BLOCK), bf16),
+        jax.ShapeDtypeStruct((HEADS, BACK, BLOCK), bf16),
         attend_scratch,
-        64 * 4 * BLOCK * BLOCK * 256,
+        20 * 64 * 4 * BLOCK * BLOCK * 256,
         3 * 2**20,
         index,
         held,
     )
-    keyval, held = lax.optimization_barrier((keyval, held))
-    from_edge = lax.ppermute(keyval, AXES, edge_pairs(count))
-    back, from_x_lo, from_x_hi = lax.optimization_barrier((back, from_x_lo, from_x_hi))
     mine = lax.all_to_all(back, AXES, 0, 0, axis_index_groups=groups, tiled=True)
     home = call(
         functools.partial(home_kernel, count=count),
         [SMEM] * 2 + [WHOLE] * 4,
         jax.ShapeDtypeStruct((HEADS, HD + 8, BLOCK), f32),
         attend_scratch,
-        32 * 4 * BLOCK * BLOCK * 256,
+        20 * 32 * 4 * BLOCK * BLOCK * 256,
         4 * 2**20,
         index,
         links,
@@ -332,6 +349,7 @@
         from_x_hi,
         from_edge,
     )
+    mine, home = lax.optimization_barrier((mine, home))
     theirs = lax.ppermute(mine, AXES, xor_pairs(count, CORE_BIT))
     return call(
         finish_kernel,

time: 92.1 us -> 80.6 us (0.88)
  waiting for transfers between devices: 33.1 us -> 21.9 us
    ppermute x1, waiting for transfers between devices: 5.13 us -> 0.01 us  [per_device(): edge = lax.ppermute(normed, AXES, edge_pairs(count))]
    all_to_all x1, starting transfers between devices: 4.67 us -> 8.66 us  [per_device(): lax.all_to_all(chunks, AXES, 0, 0, axis_index_groups=groups, tiled=True)]
    all_to_all x1, waiting for transfers between devices: 9.65 us -> 6.02 us  [per_device(): lax.all_to_all(back, AXES, 0, 0, axis_index_groups=groups, tiled=True)]
    all_to_all x1, waiting for transfers between devices: 16.7 us -> 13.9 us  [per_device(): lax.all_to_all(chunks, AXES, 0, 0, axis_index_groups=groups, tiled=True)]
    ppermute x1, starting transfers between devices: 4.14 us -> 1.92 us  [per_device(): edge = lax.ppermute(normed, AXES, edge_pairs(count))]
    ppermute x1, waiting for transfers between devices: 0.01 us -> 1.92 us  [per_device(): theirs = lax.ppermute(mine, AXES, xor_pairs(count, CORE_BIT))]
    ppermute x1, waiting for transfers between devices: 1.56 us -> 0.01 us  [per_device(): other = lax.ppermute(normed, AXES, xor_pairs(count, CORE_BIT))]
    ppermute x1, starting transfers between devices: 3.11 us -> 1.95 us  [per_device(): from_x_lo = lax.ppermute(keyval, AXES, xor_pairs(count, 3))]
  transfers between devices with their start and end apart: 7 -> 7, of which waited for: 4 -> 3; matrix products, arithmetic and copies ran while one was open for 0% -> 0% of each run, Pallas kernels for 15% -> 22%
where the time goes in v2:
time: 80.6 us; the launch traced here: 80.1 us
  starting transfers between devices  31.1 us (39%)
  waiting for transfers between devices  21.9 us (27%)
  Pallas kernels  21.5 us (27%)
  local copies, waits for them, and re-layouts  4.79 us (6%)
    pallas_call x6, Pallas kernels, call(): pl.pallas_call(kernel, in_specs=specs, out_specs=[WHOLE] * len(shapes) if...  21.5 us
    all_to_all x1, waiting for transfers between devices, per_device(): lax.all_to_all(chunks, AXES, 0, 0, axis_index_groups=groups, tiled=True)  13.9 us
    ppermute x1, starting transfers between devices, per_device(): other = lax.ppermute(normed, AXES, xor_pairs(count, CORE_BIT))  8.79 us
    all_to_all x1, starting transfers between devices, per_device(): lax.all_to_all(chunks, AXES, 0, 0, axis_index_groups=groups, tiled=True)  8.66 us
    all_to_all x1, waiting for transfers between devices, per_device(): lax.all_to_all(back, AXES, 0, 0, axis_index_groups=groups, tiled=True)  6.02 us
    unnamed x10, local copies, waits for them, and re-layouts  4.79 us
    ppermute x1, starting transfers between devices, per_device(): from_x_hi = lax.ppermute(keyval, AXES, xor_pairs(count, 5))  4.35 us
    all_to_all x1, starting transfers between devices, per_device(): lax.all_to_all(back, AXES, 0, 0, axis_index_groups=groups, tiled=True)  3.54 us
  transfers between devices with their start and end apart: 7, of which 3 were waited for; matrix products, arithmetic and copies ran while one was open for 0% of the time, Pallas kernels for 22%

profile of v2, /device:TPU:1, one launch (start us, length us, event | category | flops | bytes accessed | tf_op | source)
XLA Modules:
  0.0 80.1 jit_solution(1538225742529762088)
XLA Ops:
  0.7 0.0 copy-start
  0.7 2.4 %shard_map.55.own_ref = bf16[272,1024]{1,0:T(8,128)(2,1)} custom-call(s32[1]{0:T(128)} %bitcast.index_ref, s32[1]{0:T(128)S(6)} %copy.6.links_ref, bf16[256,1024]{1,0:T(8,128)(2,1)} %tokens_hbm.1, f32[1,1024]{1,0:T(1,128)} %bitcast.3, f32[1,1024]{1,0:T(1,128)} %bitcast.4), custom_call_target="tpu_custom_call" | custom-call | flops 12999999488 | bytes 1048576 | tf_op jit(solution)/shard_map/pallas_call | solution.py:261
  3.1 8.8 %collective-permute-start = (bf16[272,1024]{1,0:T(8,128)(2,1)}, bf16[272,1024]{1,0:T(8,128)(2,1)S(1)}, u32[]{:S(2)}, u32[]{:S(2)}) collective-permute-start(bf16[272,1024]{1,0:T(8,128)(2,1)} %shard_map.55.own_ref), channel_id=1, source_target_pairs={{0,16},{1,17},{2,18},{3,19},{4,20},{5,21},{6,22},{7,23},{8,24},{9,... | collective-permute-start | bytes 1671176 | tf_op jit(solution)/shard_map/ppermute | solution.py:297
  11.9 1.9 %collective-permute-start.1 = (bf16[272,1024]{1,0:T(8,128)(2,1)}, bf16[272,1024]{1,0:T(8,128)(2,1)S(1)}, u32[]{:S(2)}, u32[]{:S(2)}) collective-permute-start(bf16[272,1024]{1,0:T(8,128)(2,1)} %shard_map.55.own_ref), channel_id=1, source_target_pairs={{7,8},{8,7},{15,16},{16,15},{23,24},{24,23},{31,32},{32,31},{39,40... | collective-permute-start | bytes 1671176 | tf_op jit(solution)/shard_map/ppermute | solution.py:298
  13.8 0.0 collective-permute-done.other_ref
  13.8 0.0 copy-done
  13.8 0.0 copy-start.2
  13.8 1.1 %copy-done.2 = bf16[272,1024]{1,0:T(8,128)(2,1)S(1)} copy-done((bf16[272,1024]{1,0:T(8,128)(2,1)S(1)}, bf16[272,1024]{1,0:T(8,128)(2,1)}, u32[]{:S(2)}) %copy-start.2) | copy-done | bytes 557080
  14.9 3.1 %shard_map.56 = (bf16[8,392,256]{2,1,0:T(8,128)(2,1)}, bf16[8,128,256]{2,1,0:T(8,128)(2,1)S(1)}) custom-call(s32[1]{0:T(128)} %bitcast.index_ref, s32[1]{0:T(128)S(6)} %copy.6.links_ref, bf16[272,1024]{1,0:T(8,128)(2,1)S(1)} %copy-done.2, bf16[272,1024]{1,0:T(8,128)(2,1)S(1)} %collective-permute-done.other_ref, bf16[1024,1536]{1,0:T(8,128)(2,1)S(1)} %copy-done), custom_call_target="tpu_custom_call" | custom-call | flops 32212254720 | bytes 6291456 | tf_op jit(solution)/shard_map/pallas_call | solution.py:261
  18.0 8.7 %all-to-all-start = ((bf16[8,392,256]{2,1,0:T(8,128)(2,1)}), bf16[8,392,256]{2,1,0:T(8,128)(2,1)S(1)}, u32[]{:S(2)}, u32[]{:S(2)}) async-start(bf16[8,392,256]{2,1,0:T(8,128)(2,1)} %get-tuple-element.13.chunk_ref), calls=%async_computation | async-start | bytes 3211264 | tf_op jit(solution)/shard_map/all_to_all | solution.py:312
  26.7 0.0 collective-permute-done.1.normed_ref
  26.7 0.0 copy-start.1
  26.7 1.9 %copy-done.1 = bf16[1024,1536]{1,0:T(8,128)(2,1)S(1)} copy-done((bf16[1024,1536]{1,0:T(8,128)(2,1)S(1)}, bf16[1024,1536]{1,0:T(8,128)(2,1)}, u32[]{:S(2)}) %copy-start.1) | copy-done | bytes 3145752
  28.6 0.8 %shard_map.57.edge_ref = bf16[8,128,256]{2,1,0:T(8,128)(2,1)S(1)} custom-call(bf16[272,1024]{1,0:T(8,128)(2,1)S(1)} %collective-permute-done.1.normed_ref, bf16[1024,1536]{1,0:T(8,128)(2,1)S(1)} %copy-done.1), custom_call_target="tpu_custom_call" | custom-call | flops 32212254720 | bytes 4194304 | tf_op jit(solution)/shard_map/pallas_call | solution.py:261
  29.4 0.0 copy-start.3
  29.4 0.8 copy-done.3
  30.2 4.3 %collective-permute-start.3 = (bf16[8,128,256]{2,1,0:T(8,128)(2,1)S(1)}, bf16[8,128,256]{2,1,0:T(8,128)(2,1)S(1)}, u32[]{:S(2)}, u32[]{:S(2)}) collective-permute-start(bf16[8,128,256]{2,1,0:T(8,128)(2,1)S(1)} %get-tuple-element.17), channel_id=1, source_target_pairs={{0,32},{1,33},{2,34},{3,35},{4,36},{5,37},{6,38},{7,39},{8,40},{9,... | collective-permute-start | bytes 1572872 | tf_op jit(solution)/shard_map/ppermute | solution.py:325
  34.5 2.0 %collective-permute-start.2 = (bf16[8,128,256]{2,1,0:T(8,128)(2,1)S(1)}, bf16[8,128,256]{2,1,0:T(8,128)(2,1)S(1)}, u32[]{:S(2)}, u32[]{:S(2)}) collective-permute-start(bf16[8,128,256]{2,1,0:T(8,128)(2,1)S(1)} %get-tuple-element.17), channel_id=1, source_target_pairs={{0,8},{1,9},{2,10},{3,11},{4,12},{5,13},{6,14},{7,15},{8,0},{9,1},... | collective-permute-start | bytes 1572872 | tf_op jit(solution)/shard_map/ppermute | solution.py:324
  36.5 13.9 %all-to-all-done.held_ref = bf16[8,392,256]{2,1,0:T(8,128)(2,1)S(1)} async-done(((bf16[8,392,256]{2,1,0:T(8,128)(2,1)}), bf16[8,392,256]{2,1,0:T(8,128)(2,1)S(1)}, u32[]{:S(2)}, u32[]{:S(2)}) %all-to-all-start) | async-done | bytes 1605664 | tf_op jit(solution)/shard_map/all_to_all | solution.py:312
  50.4 8.8 %shard_map.58 = bf16[8,136,256]{2,1,0:T(8,128)(2,1)} custom-call(s32[1]{0:T(128)} %bitcast.index_ref, bf16[8,392,256]{2,1,0:T(8,128)(2,1)S(1)} %all-to-all-done.held_ref), custom_call_target="tpu_custom_call" | custom-call | flops 85899345920 | bytes 3145728 | tf_op jit(solution)/shard_map/pallas_call | solution.py:261
  59.2 3.5 %all-to-all-start.1 = ((bf16[8,136,256]{2,1,0:T(8,128)(2,1)}), bf16[8,136,256]{2,1,0:T(8,128)(2,1)S(1)}, u32[]{:S(2)}, u32[]{:S(2)}) async-start(bf16[8,136,256]{2,1,0:T(8,128)(2,1)} %shard_map.58), calls=%async_computation.1 | async-start | bytes 1114112 | tf_op jit(solution)/shard_map/all_to_all | solution.py:337
  62.8 0.0 collective-permute-done.3.x_hi_ref
  62.8 0.0 collective-permute-done.2.x_lo_ref
  62.8 0.0 copy-start.4
  62.8 1.0 %copy-done.4 = bf16[8,128,256]{2,1,0:T(8,128)(2,1)S(1)} copy-done((bf16[8,128,256]{2,1,0:T(8,128)(2,1)S(1)}, bf16[8,128,256]{2,1,0:T(8,128)(2,1)}, u32[]{:S(2)}) %copy-start.4) | copy-done | bytes 524312
  63.9 5.3 %shard_map.59.home_ref = f32[8,72,256]{2,1,0:T(8,128)S(1)} custom-call(s32[1]{0:T(128)} %bitcast.index_ref, s32[1]{0:T(128)S(6)} %copy.6.links_ref, bf16[8,392,256]{2,1,0:T(8,128)(2,1)} %get-tuple-element.13.chunk_ref, bf16[8,128,256]{2,1,0:T(8,128)(2,1)S(1)} %collective-permute-done.2.x_lo_ref, bf16[8,128,256]{2,1,0:T(8,128)(2,1)S(1)} %collective-permute-done.3.x_hi_ref, ...), custom_call_target="tpu_custom_call" | custom-call | flops 42949672960 | bytes 4194304 | tf_op jit(solution)/shard_map/pallas_call | solution.py:261
  69.2 6.0 %all-to-all-done.1.own_ref = bf16[8,136,256]{2,1,0:T(8,128)(2,1)S(1)} async-done(((bf16[8,136,256]{2,1,0:T(8,128)(2,1)}), bf16[8,136,256]{2,1,0:T(8,128)(2,1)S(1)}, u32[]{:S(2)}, u32[]{:S(2)}) %all-to-all-start.1) | async-done | bytes 557088 | tf_op jit(solution)/shard_map/all_to_all | solution.py:337
  75.2 1.9 %collective-permute-start.4 = (bf16[8,136,256]{2,1,0:T(8,128)(2,1)S(1)}, bf16[8,136,256]{2,1,0:T(8,128)(2,1)S(1)}, u32[]{:S(2)}, u32[]{:S(2)}) collective-permute-start(bf16[8,136,256]{2,1,0:T(8,128)(2,1)S(1)} %all-to-all-done.1.own_ref), channel_id=1, source_target_pairs={{0,16},{1,17},{2,18},{3,19},{4,20},{5,21},{6,22},{7,23},{8,24},{9,... | collective-permute-start | bytes 1671176 | tf_op jit(solution)/shard_map/ppermute | solution.py:353
  77.1 1.9 %collective-permute-done.4.other_ref = bf16[8,136,256]{2,1,0:T(8,128)(2,1)S(1)} collective-permute-done((bf16[8,136,256]{2,1,0:T(8,128)(2,1)S(1)}, bf16[8,136,256]{2,1,0:T(8,128)(2,1)S(1)}, u32[]{:S(2)}, u32[]{:S(2)}) %collective-permute-start.4) | collective-permute-done | bytes 557088 | tf_op jit(solution)/shard_map/ppermute | solution.py:353
  79.0 1.1 %shard_map.60 = f32[256,512]{1,0:T(8,128)} custom-call(f32[8,72,256]{2,1,0:T(8,128)S(1)} %shard_map.59.home_ref, bf16[8,136,256]{2,1,0:T(8,128)(2,1)S(1)} %all-to-all-done.1.own_ref, bf16[8,136,256]{2,1,0:T(8,128)(2,1)S(1)} %collective-permute-done.4.other_ref), custom_call_target="tpu_custom_call" | custom-call | flops 10000000 | bytes 2097152 | tf_op jit(solution)/shard_map/pallas_call | solution.py:261
Async XLA Ops:
  0.7 13.2 %copy-start = (bf16[1024,1536]{1,0:T(8,128)(2,1)S(1)}, bf16[1024,1536]{1,0:T(8,128)(2,1)}, u32[]{:S(2)}) copy-start(bf16[1024,1536]{1,0:T(8,128)(2,1)} %w_ref.3) | copy-start | bytes 9437188
  3.1 10.7 %collective-permute-start = (bf16[272,1024]{1,0:T(8,128)(2,1)}, bf16[272,1024]{1,0:T(8,128)(2,1)S(1)}, u32[]{:S(2)}, u32[]{:S(2)}) collective-permute-start(bf16[272,1024]{1,0:T(8,128)(2,1)} %shard_map.55.own_ref), channel_id=1, source_target_pairs={{0,16},{1,17},{2,18},{3,19},{4,20},{5,21},{6,22},{7,23},{8,24},{9,... | collective-permute-start | bytes 1671176 | tf_op jit(solution)/shard_map/ppermute | solution.py:297
  11.9 14.8 %collective-permute-start.1 = (bf16[272,1024]{1,0:T(8,128)(2,1)}, bf16[272,1024]{1,0:T(8,128)(2,1)S(1)}, u32[]{:S(2)}, u32[]{:S(2)}) collective-permute-start(bf16[272,1024]{1,0:T(8,128)(2,1)} %shard_map.55.own_ref), channel_id=1, source_target_pairs={{7,8},{8,7},{15,16},{16,15},{23,24},{24,23},{31,32},{32,31},{39,40... | collective-permute-start | bytes 1671176 | tf_op jit(solution)/shard_map/ppermute | solution.py:298
  13.8 1.1 %copy-start.2 = (bf16[272,1024]{1,0:T(8,128)(2,1)S(1)}, bf16[272,1024]{1,0:T(8,128)(2,1)}, u32[]{:S(2)}) copy-start(bf16[272,1024]{1,0:T(8,128)(2,1)} %shard_map.55.own_ref) | copy-start | bytes 1671172
  18.0 32.4 %all-to-all-start = ((bf16[8,392,256]{2,1,0:T(8,128)(2,1)}), bf16[8,392,256]{2,1,0:T(8,128)(2,1)S(1)}, u32[]{:S(2)}, u32[]{:S(2)}) async-start(bf16[8,392,256]{2,1,0:T(8,128)(2,1)} %get-tuple-element.13.chunk_ref), calls=%async_computation | async-start | bytes 3211264 | tf_op jit(solution)/shard_map/all_to_all | solution.py:312
  26.7 1.9 %copy-start.1 = (bf16[1024,1536]{1,0:T(8,128)(2,1)S(1)}, bf16[1024,1536]{1,0:T(8,128)(2,1)}, u32[]{:S(2)}) copy-start(bf16[1024,1536]{1,0:T(8,128)(2,1)} %w_ref.3) | copy-start | bytes 9437188
  29.4 0.8 copy-start.3
  30.2 32.6 %collective-permute-start.3 = (bf16[8,128,256]{2,1,0:T(8,128)(2,1)S(1)}, bf16[8,128,256]{2,1,0:T(8,128)(2,1)S(1)}, u32[]{:S(2)}, u32[]{:S(2)}) collective-permute-start(bf16[8,128,256]{2,1,0:T(8,128)(2,1)S(1)} %get-tuple-element.17), channel_id=1, source_target_pairs={{0,32},{1,33},{2,34},{3,35},{4,36},{5,37},{6,38},{7,39},{8,40},{9,... | collective-permute-start | bytes 1572872 | tf_op jit(solution)/shard_map/ppermute | solution.py:325
  34.5 28.3 %collective-permute-start.2 = (bf16[8,128,256]{2,1,0:T(8,128)(2,1)S(1)}, bf16[8,128,256]{2,1,0:T(8,128)(2,1)S(1)}, u32[]{:S(2)}, u32[]{:S(2)}) collective-permute-start(bf16[8,128,256]{2,1,0:T(8,128)(2,1)S(1)} %get-tuple-element.17), channel_id=1, source_target_pairs={{0,8},{1,9},{2,10},{3,11},{4,12},{5,13},{6,14},{7,15},{8,0},{9,1},... | collective-permute-start | bytes 1572872 | tf_op jit(solution)/shard_map/ppermute | solution.py:324
  59.2 15.9 %all-to-all-start.1 = ((bf16[8,136,256]{2,1,0:T(8,128)(2,1)}), bf16[8,136,256]{2,1,0:T(8,128)(2,1)S(1)}, u32[]{:S(2)}, u32[]{:S(2)}) async-start(bf16[8,136,256]{2,1,0:T(8,128)(2,1)} %shard_map.58), calls=%async_computation.1 | async-start | bytes 1114112 | tf_op jit(solution)/shard_map/all_to_all | solution.py:337
  62.8 1.0 %copy-start.4 = (bf16[8,128,256]{2,1,0:T(8,128)(2,1)S(1)}, bf16[8,128,256]{2,1,0:T(8,128)(2,1)}, u32[]{:S(2)}) copy-start(bf16[8,128,256]{2,1,0:T(8,128)(2,1)} %copy-done.3) | copy-start | bytes 1572868
  75.2 3.8 %collective-permute-start.4 = (bf16[8,136,256]{2,1,0:T(8,128)(2,1)S(1)}, bf16[8,136,256]{2,1,0:T(8,128)(2,1)S(1)}, u32[]{:S(2)}, u32[]{:S(2)}) collective-permute-start(bf16[8,136,256]{2,1,0:T(8,128)(2,1)S(1)} %all-to-all-done.1.own_ref), channel_id=1, source_target_pairs={{0,16},{1,17},{2,18},{3,19},{4,20},{5,21},{6,22},{7,23},{8,24},{9,... | collective-permute-start | bytes 1671176 | tf_op jit(solution)/shard_map/ppermute | solution.py:353

commit v3 on v2

--- a/solution.py
+++ b/solution.py
@@ -24,7 +24,6 @@
 Y_COUNT = 8
 CORE_BIT = 4
 VMEM_LIMIT = 32 * 1024 * 1024
-WIDE_LIMIT = 56 * 1024 * 1024
 
 
 def fields(index):
@@ -87,27 +86,17 @@
     return table
 
 
-def norm_kernel(index_ref, links_ref, tokens_hbm, gain_hbm, shift_hbm, out_ref, tokens_ref, gain_ref, shift_ref, sems):
-    copies = [
-        pltpu.make_async_copy(source, target, sems.at[at])
-        for at, (source, target) in enumerate(
-            ((tokens_hbm, tokens_ref), (gain_hbm, gain_ref), (shift_hbm, shift_ref))
-        )
-    ]
-    for copy in copies:
-        copy.start()
+def norm_kernel(index_ref, links_ref, tokens_ref, affine_ref, out_ref):
     index = index_ref[0]
     times = key_times(index, links_ref[0], 1 - ((index >> CORE_BIT) & 1))
     out_ref[BLOCK:, :] = stack_rows(times, 16, out_ref.shape[1], jnp.int32).astype(jnp.float32).astype(jnp.bfloat16)
-    for copy in copies:
-        copy.wait()
-    out_ref[:BLOCK, :] = normalize(tokens_ref[...], gain_ref[...], shift_ref[...])
-
-
-def project(normed_ref, w_ref, kinds, store):
+    out_ref[:BLOCK, :] = normalize(tokens_ref[...], affine_ref[0:1, :], affine_ref[1:2, :])
+
+
+def project(normed_ref, w_ref, kinds, store, starts=(0, 4 * HD)):
     tile = 4 * HD
     for kind in kinds:
-        for start in range(0, INNER, tile):
+        for start in starts:
             columns = w_ref[:, kind * INNER + start : kind * INNER + start + tile]
             product = jnp.dot(normed_ref[...], columns, preferred_element_type=jnp.float32)
             turned = product.T.astype(jnp.bfloat16)
@@ -115,7 +104,7 @@
                 store(kind, start // HD + local, turned[local * HD : (local + 1) * HD])
 
 
-def project_kernel(index_ref, links_ref, own_ref, other_ref, w_ref, chunk_ref, keyval_ref, normed_ref):
+def project_kernel(index_ref, links_ref, own_ref, other_ref, w_ref, chunk_hbm, keyval_ref, normed_ref, chunk_ref, sems):
     index = index_ref[0]
     times = key_times(index, links_ref[0], (index >> CORE_BIT) & 1)
     table = stack_rows(times, 8, BLOCK, jnp.int32).astype(jnp.float32)
@@ -135,7 +124,15 @@
         if kind > 0:
             keyval_ref[head, (kind - 1) * HD : kind * HD, :] = rows[:, :BLOCK]
 
-    project(normed_ref, w_ref, (0, 1, 2), store)
+    half = HEADS // 2
+    sends = []
+    for at in range(2):
+        project(normed_ref, w_ref, (0, 1, 2), store, (at * half * HD,))
+        heads = pl.ds(at * half, half)
+        sends.append(pltpu.make_async_copy(chunk_ref.at[heads], chunk_hbm.at[heads], sems.at[at]))
+        sends[-1].start()
+    for send in sends:
+        send.wait()
 
 
 def edge_kernel(normed_ref, w_ref, keyval_ref):
@@ -145,9 +142,11 @@
     project(normed_ref.at[pl.ds(0, BLOCK)], w_ref, (1, 2), store)
 
 
-def attend_all(items, score_ref, weight_ref):
+def attend_all(items, score_ref, weight_ref, key_dim=0):
     for at, (query, key, _) in enumerate(items):
-        score_ref[at] = lax.dot_general(key(), query(), (((0,), (0,)), ((), ())), preferred_element_type=jnp.float32)
+        score_ref[at] = lax.dot_general(
+            key(), query(), (((key_dim,), (0,)), ((), ())), preferred_element_type=jnp.float32
+        )
     stats = []
     for at in range(len(items)):
         scores = score_ref[at]
@@ -180,19 +179,24 @@
     return [high, middle, rest - middle]
 
 
-def group_kernel(index_ref, held_ref, back_ref, score_ref, weight_ref):
+def group_kernel(index_ref, held_ref, back_hbm, score_ref, weight_ref, key_ref, back_ref, sems):
     core = (index_ref[0] >> CORE_BIT) & 1
+    for source in range(HEADS):
+        for slot in range(SLOTS):
+            start = slot * WIDE + HD
+            key_ref[source, slot] = held_ref[source, start : start + HD, :].T
 
     def step(member, carry):
         table = held_ref[member, SLOTS * WIDE :, :].astype(jnp.float32)
         sources = key_members(member, core)
         load = lambda source, start: lambda: held_ref[source, start : start + HD, :]
+        turned = lambda source, slot: lambda: key_ref[source, slot]
         items = [
-            (load(member, slot * WIDE), load(source, slot * WIDE + HD), load(source, slot * WIDE + 2 * HD))
+            (load(member, slot * WIDE), turned(source, slot), load(source, slot * WIDE + 2 * HD))
             for slot in range(SLOTS)
             for source in sources
         ]
-        results = attend_all(items, score_ref, weight_ref)
+        results = attend_all(items, score_ref, weight_ref, 1)
         stats = []
         for slot in range(SLOTS):
             at = slot * KEYS
@@ -202,9 +206,12 @@
             back_ref[member, slot * HD : (slot + 1) * HD, :] = (accum / total).astype(jnp.bfloat16)
             stats.extend(thirds(top + jnp.log(total)))
         back_ref[member, SLOTS * HD :, :] = stack_rows(stats, 8, BLOCK).astype(jnp.bfloat16)
+        pltpu.make_async_copy(back_ref.at[member], back_hbm.at[member], sems.at[member]).start()
         return carry
 
     lax.fori_loop(0, HEADS, step, 0)
+    for member in range(HEADS):
+        pltpu.make_async_copy(back_ref.at[member], back_hbm.at[member], sems.at[member]).wait()
 
 
 def home_kernel(index_ref, links_ref, chunk_ref, x_lo_ref, x_hi_ref, edge_ref, out_ref, score_ref, weight_ref, count):
@@ -257,11 +264,11 @@
 HBM = pl.BlockSpec(memory_space=pltpu.HBM)
 
 
-def call(kernel, specs, shapes, scratch, flops, moved, *operands, limit=VMEM_LIMIT):
+def call(kernel, specs, shapes, scratch, flops, moved, *operands, limit=VMEM_LIMIT, outs=None):
     return pl.pallas_call(
         kernel,
         in_specs=specs,
-        out_specs=[WHOLE] * len(shapes) if isinstance(shapes, list) else WHOLE,
+        out_specs=outs or ([WHOLE] * len(shapes) if isinstance(shapes, list) else WHOLE),
         out_shape=shapes,
         scratch_shapes=scratch,
         compiler_params=pltpu.CompilerParams(vmem_limit_bytes=limit),
@@ -277,22 +284,15 @@
     attend_scratch = [pltpu.VMEM((2 * KEYS, BLOCK, BLOCK), f32), pltpu.VMEM((2 * KEYS, BLOCK, BLOCK), bf16)]
     normed = call(
         norm_kernel,
-        [SMEM] * 2 + [HBM] * 3,
+        [SMEM] * 2 + [WHOLE] * 2,
         jax.ShapeDtypeStruct((BLOCK + 16, width), bf16),
-        [
-            pltpu.VMEM((BLOCK, width), bf16),
-            pltpu.VMEM((1, width), f32),
-            pltpu.VMEM((1, width), f32),
-            pltpu.SemaphoreType.DMA((3,)),
-        ],
+        [],
         13 * 10**9,
         2**20,
         index,
         links,
         tokens,
-        norm_gain[None, :],
-        norm_shift[None, :],
-        limit=WIDE_LIMIT,
+        jnp.stack([norm_gain, norm_shift]),
     )
     other = lax.ppermute(normed, AXES, xor_pairs(count, CORE_BIT))
     edge = lax.ppermute(normed, AXES, edge_pairs(count))
@@ -300,7 +300,11 @@
         project_kernel,
         [SMEM] * 2 + [WHOLE] * 3,
         [jax.ShapeDtypeStruct((HEADS, CHUNK, BLOCK), bf16), jax.ShapeDtypeStruct((HEADS, 2 * HD, BLOCK), bf16)],
-        [pltpu.VMEM((2 * BLOCK, width), bf16)],
+        [
+            pltpu.VMEM((2 * BLOCK, width), bf16),
+            pltpu.VMEM((HEADS, CHUNK, BLOCK), bf16),
+            pltpu.SemaphoreType.DMA((2,)),
+        ],
         20 * 2 * 2 * BLOCK * w_qkv.shape[0] * w_qkv.shape[1],
         6 * 2**20,
         index,
@@ -308,6 +312,7 @@
         normed,
         other,
         w_qkv,
+        outs=[HBM, WHOLE],
     )
     held = lax.all_to_all(chunks, AXES, 0, 0, axis_index_groups=groups, tiled=True)
     from_edge = call(
@@ -328,11 +333,13 @@
         group_kernel,
         [SMEM, WHOLE],
         jax.ShapeDtypeStruct((HEADS, BACK, BLOCK), bf16),
-        attend_scratch,
+        attend_scratch
+        + [pltpu.VMEM((HEADS, SLOTS, BLOCK, HD), bf16), pltpu.VMEM((HEADS, BACK, BLOCK), bf16), pltpu.SemaphoreType.DMA((HEADS,))],
         20 * 64 * 4 * BLOCK * BLOCK * 256,
         3 * 2**20,
         index,
         held,
+        outs=HBM,
     )
     mine = lax.all_to_all(back, AXES, 0, 0, axis_index_groups=groups, tiled=True)
     home = call(

time: 80.6 us -> 78.9 us (0.979)
  starting transfers between devices: 31.1 us -> 35.6 us
  waiting for transfers between devices: 21.9 us -> 17.6 us
  Pallas kernels: 21.5 us -> 18.9 us
    all_to_all x1, waiting for transfers between devices: 13.9 us -> 9.32 us  [per_device(): lax.all_to_all(chunks, AXES, 0, 0, axis_index_groups=groups, tiled=True)]
    ppermute x1, starting transfers between devices: 4.35 us -> 8.64 us  [per_device(): from_x_hi = lax.ppermute(keyval, AXES, xor_pairs(count, 5))]
    pallas_call x6, Pallas kernels: 21.5 us -> 18.9 us  [call(): pl.pallas_call(kernel, in_specs=specs, out_specs=outs or ([WHOLE] * len(s...]
  transfers between devices with their start and end apart: 7 -> 7, of which waited for: 3 -> 4; matrix products, arithmetic and copies ran while one was open for 0% -> 0% of each run, Pallas kernels for 22% -> 22%
where the time goes in v3:
time: 78.9 us; the launch traced here: 78.3 us
  starting transfers between devices  35.6 us (45%)
  Pallas kernels  18.9 us (24%)
  waiting for transfers between devices  17.6 us (22%)
  local copies, waits for them, and re-layouts  4.75 us (6%)
  between operations  0.8 us (1%)
    pallas_call x6, Pallas kernels, call(): pl.pallas_call(kernel, in_specs=specs, out_specs=outs or ([WHOLE] * len(s...  18.9 us
    all_to_all x1, waiting for transfers between devices, per_device(): lax.all_to_all(chunks, AXES, 0, 0, axis_index_groups=groups, tiled=True)  9.32 us
    ppermute x1, starting transfers between devices, per_device(): other = lax.ppermute(normed, AXES, xor_pairs(count, CORE_BIT))  8.92 us
    all_to_all x1, starting transfers between devices, per_device(): lax.all_to_all(chunks, AXES, 0, 0, axis_index_groups=groups, tiled=True)  8.68 us
    ppermute x1, starting transfers between devices, per_device(): from_x_hi = lax.ppermute(keyval, AXES, xor_pairs(count, 5))  8.64 us
    all_to_all x1, waiting for transfers between devices, per_device(): lax.all_to_all(back, AXES, 0, 0, axis_index_groups=groups, tiled=True)  6.01 us
    unnamed x10, local copies, waits for them, and re-layouts  4.75 us
    all_to_all x1, starting transfers between devices, per_device(): lax.all_to_all(back, AXES, 0, 0, axis_index_groups=groups, tiled=True)  3.55 us
  transfers between devices with their start and end apart: 7, of which 4 were waited for; matrix products, arithmetic and copies ran while one was open for 0% of the time, Pallas kernels for 22%

profile of v3, /device:TPU:1, one launch (start us, length us, event | category | flops | bytes accessed | tf_op | source)
XLA Modules:
  0.0 78.3 jit_solution(15602771968905003912)
XLA Ops:
  0.7 0.7 pad_maximum_fusion.affine_ref
  1.4 0.0 copy-start.2
  1.4 1.0 %copy-done.2 = bf16[256,1024]{1,0:T(8,128)(2,1)S(1)} copy-done((bf16[256,1024]{1,0:T(8,128)(2,1)S(1)}, bf16[256,1024]{1,0:T(8,128)(2,1)}, u32[]{:S(2)}) %copy-start.2) | copy-done | bytes 524312
  2.4 0.0 copy-start
  2.4 0.4 shard_map.55.own_ref
  2.8 8.9 %collective-permute-start = (bf16[272,1024]{1,0:T(8,128)(2,1)S(1)}, bf16[272,1024]{1,0:T(8,128)(2,1)S(1)}, u32[]{:S(2)}, u32[]{:S(2)}) collective-permute-start(bf16[272,1024]{1,0:T(8,128)(2,1)S(1)} %shard_map.55.own_ref), channel_id=1, source_target_pairs={{0,16},{1,17},{2,18},{3,19},{4,20},{5,21},{6,22},{7,23},{8,24},{9,... | collective-permute-start | bytes 1671176 | tf_op jit(solution)/shard_map/ppermute | solution.py:297
  11.7 1.9 %collective-permute-start.1 = (bf16[272,1024]{1,0:T(8,128)(2,1)S(1)}, bf16[272,1024]{1,0:T(8,128)(2,1)S(1)}, u32[]{:S(2)}, u32[]{:S(2)}) collective-permute-start(bf16[272,1024]{1,0:T(8,128)(2,1)S(1)} %shard_map.55.own_ref), channel_id=1, source_target_pairs={{7,8},{8,7},{15,16},{16,15},{23,24},{24,23},{31,32},{32,31},{39,40... | collective-permute-start | bytes 1671176 | tf_op jit(solution)/shard_map/ppermute | solution.py:298
  13.7 0.0 collective-permute-done.other_ref
  13.7 0.0 copy-done
  13.7 2.9 %shard_map.56 = (bf16[8,392,256]{2,1,0:T(8,128)(2,1)}, bf16[8,128,256]{2,1,0:T(8,128)(2,1)S(1)}) custom-call(s32[1]{0:T(128)} %bitcast.index_ref, s32[1]{0:T(128)S(6)} %copy.6.links_ref, bf16[272,1024]{1,0:T(8,128)(2,1)S(1)} %shard_map.55.own_ref, bf16[272,1024]{1,0:T(8,128)(2,1)S(1)} %collective-permute-done.other_ref, bf16[1024,1536]{1,0:T(8,128)(2,1)S(1)} %copy-done), custom_call_target="tpu_custom_call" | custom-call | flops 32212254720 | bytes 6291456 | tf_op jit(solution)/shard_map/pallas_call | solution.py:268
  16.6 8.7 %all-to-all-start = ((bf16[8,392,256]{2,1,0:T(8,128)(2,1)}), bf16[8,392,256]{2,1,0:T(8,128)(2,1)S(1)}, u32[]{:S(2)}, u32[]{:S(2)}) async-start(bf16[8,392,256]{2,1,0:T(8,128)(2,1)} %get-tuple-element.13.chunk_ref), calls=%async_computation | async-start | bytes 3211264 | tf_op jit(solution)/shard_map/all_to_all | solution.py:317
  25.2 0.3 collective-permute-done.1.normed_ref
  25.6 0.0 copy-start.1
  25.6 1.9 %copy-done.1 = bf16[1024,1536]{1,0:T(8,128)(2,1)S(1)} copy-done((bf16[1024,1536]{1,0:T(8,128)(2,1)S(1)}, bf16[1024,1536]{1,0:T(8,128)(2,1)}, u32[]{:S(2)}) %copy-start.1) | copy-done | bytes 3145752
  27.5 0.8 %shard_map.57.edge_ref = bf16[8,128,256]{2,1,0:T(8,128)(2,1)S(1)} custom-call(bf16[272,1024]{1,0:T(8,128)(2,1)S(1)} %collective-permute-done.1.normed_ref, bf16[1024,1536]{1,0:T(8,128)(2,1)S(1)} %copy-done.1), custom_call_target="tpu_custom_call" | custom-call | flops 32212254720 | bytes 4194304 | tf_op jit(solution)/shard_map/pallas_call | solution.py:268
  28.3 0.0 copy-start.3
  28.3 0.8 %copy-done.3 = bf16[8,128,256]{2,1,0:T(8,128)(2,1)} copy-done((bf16[8,128,256]{2,1,0:T(8,128)(2,1)}, bf16[8,128,256]{2,1,0:T(8,128)(2,1)S(1)}, u32[]{:S(2)}) %copy-start.3) | copy-done | bytes 524312
  29.1 8.6 %collective-permute-start.3 = (bf16[8,128,256]{2,1,0:T(8,128)(2,1)S(1)}, bf16[8,128,256]{2,1,0:T(8,128)(2,1)S(1)}, u32[]{:S(2)}, u32[]{:S(2)}) collective-permute-start(bf16[8,128,256]{2,1,0:T(8,128)(2,1)S(1)} %get-tuple-element.17), channel_id=1, source_target_pairs={{0,32},{1,33},{2,34},{3,35},{4,36},{5,37},{6,38},{7,39},{8,40},{9,... | collective-permute-start | bytes 1572872 | tf_op jit(solution)/shard_map/ppermute | solution.py:330
  37.7 2.0 %collective-permute-start.2 = (bf16[8,128,256]{2,1,0:T(8,128)(2,1)S(1)}, bf16[8,128,256]{2,1,0:T(8,128)(2,1)S(1)}, u32[]{:S(2)}, u32[]{:S(2)}) collective-permute-start(bf16[8,128,256]{2,1,0:T(8,128)(2,1)S(1)} %get-tuple-element.17), channel_id=1, source_target_pairs={{0,8},{1,9},{2,10},{3,11},{4,12},{5,13},{6,14},{7,15},{8,0},{9,1},... | collective-permute-start | bytes 1572872 | tf_op jit(solution)/shard_map/ppermute | solution.py:329
  39.7 9.3 %all-to-all-done.held_ref = bf16[8,392,256]{2,1,0:T(8,128)(2,1)S(1)} async-done(((bf16[8,392,256]{2,1,0:T(8,128)(2,1)}), bf16[8,392,256]{2,1,0:T(8,128)(2,1)S(1)}, u32[]{:S(2)}, u32[]{:S(2)}) %all-to-all-start) | async-done | bytes 1605664 | tf_op jit(solution)/shard_map/all_to_all | solution.py:317
  49.0 8.4 %shard_map.58 = bf16[8,136,256]{2,1,0:T(8,128)(2,1)} custom-call(s32[1]{0:T(128)} %bitcast.index_ref, bf16[8,392,256]{2,1,0:T(8,128)(2,1)S(1)} %all-to-all-done.held_ref), custom_call_target="tpu_custom_call" | custom-call | flops 85899345920 | bytes 3145728 | tf_op jit(solution)/shard_map/pallas_call | solution.py:268
  57.5 3.5 %all-to-all-start.1 = ((bf16[8,136,256]{2,1,0:T(8,128)(2,1)}), bf16[8,136,256]{2,1,0:T(8,128)(2,1)S(1)}, u32[]{:S(2)}, u32[]{:S(2)}) async-start(bf16[8,136,256]{2,1,0:T(8,128)(2,1)} %shard_map.58), calls=%async_computation.1 | async-start | bytes 1114112 | tf_op jit(solution)/shard_map/all_to_all | solution.py:344
  61.0 0.0 collective-permute-done.3.x_hi_ref
  61.0 0.0 collective-permute-done.2.x_lo_ref
  61.0 0.0 copy-start.4
  61.0 1.0 %copy-done.4 = bf16[8,128,256]{2,1,0:T(8,128)(2,1)S(1)} copy-done((bf16[8,128,256]{2,1,0:T(8,128)(2,1)S(1)}, bf16[8,128,256]{2,1,0:T(8,128)(2,1)}, u32[]{:S(2)}) %copy-start.4) | copy-done | bytes 524312
  62.1 5.3 %shard_map.59.home_ref = f32[8,72,256]{2,1,0:T(8,128)S(1)} custom-call(s32[1]{0:T(128)} %bitcast.index_ref, s32[1]{0:T(128)S(6)} %copy.6.links_ref, bf16[8,392,256]{2,1,0:T(8,128)(2,1)} %get-tuple-element.13.chunk_ref, bf16[8,128,256]{2,1,0:T(8,128)(2,1)S(1)} %collective-permute-done.2.x_lo_ref, bf16[8,128,256]{2,1,0:T(8,128)(2,1)S(1)} %collective-permute-done.3.x_hi_ref, ...), custom_call_target="tpu_custom_call" | custom-call | flops 42949672960 | bytes 4194304 | tf_op jit(solution)/shard_map/pallas_call | solution.py:268
  67.4 6.0 %all-to-all-done.1.own_ref = bf16[8,136,256]{2,1,0:T(8,128)(2,1)S(1)} async-done(((bf16[8,136,256]{2,1,0:T(8,128)(2,1)}), bf16[8,136,256]{2,1,0:T(8,128)(2,1)S(1)}, u32[]{:S(2)}, u32[]{:S(2)}) %all-to-all-start.1) | async-done | bytes 557088 | tf_op jit(solution)/shard_map/all_to_all | solution.py:344
  73.4 1.9 %collective-permute-start.4 = (bf16[8,136,256]{2,1,0:T(8,128)(2,1)S(1)}, bf16[8,136,256]{2,1,0:T(8,128)(2,1)S(1)}, u32[]{:S(2)}, u32[]{:S(2)}) collective-permute-start(bf16[8,136,256]{2,1,0:T(8,128)(2,1)S(1)} %all-to-all-done.1.own_ref), channel_id=1, source_target_pairs={{0,16},{1,17},{2,18},{3,19},{4,20},{5,21},{6,22},{7,23},{8,24},{9,... | collective-permute-start | bytes 1671176 | tf_op jit(solution)/shard_map/ppermute | solution.py:360
  75.3 1.9 %collective-permute-done.4.other_ref = bf16[8,136,256]{2,1,0:T(8,128)(2,1)S(1)} collective-permute-done((bf16[8,136,256]{2,1,0:T(8,128)(2,1)S(1)}, bf16[8,136,256]{2,1,0:T(8,128)(2,1)S(1)}, u32[]{:S(2)}, u32[]{:S(2)}) %collective-permute-start.4) | collective-permute-done | bytes 557088 | tf_op jit(solution)/shard_map/ppermute | solution.py:360
  77.3 1.1 %shard_map.60 = f32[256,512]{1,0:T(8,128)} custom-call(f32[8,72,256]{2,1,0:T(8,128)S(1)} %shard_map.59.home_ref, bf16[8,136,256]{2,1,0:T(8,128)(2,1)S(1)} %all-to-all-done.1.own_ref, bf16[8,136,256]{2,1,0:T(8,128)(2,1)S(1)} %collective-permute-done.4.other_ref), custom_call_target="tpu_custom_call" | custom-call | flops 10000000 | bytes 2097152 | tf_op jit(solution)/shard_map/pallas_call | solution.py:268
Async XLA Ops:
  1.4 1.0 %copy-start.2 = (bf16[256,1024]{1,0:T(8,128)(2,1)S(1)}, bf16[256,1024]{1,0:T(8,128)(2,1)}, u32[]{:S(2)}) copy-start(bf16[256,1024]{1,0:T(8,128)(2,1)} %tokens_ref.1) | copy-start | bytes 1572868
  2.4 11.3 %copy-start = (bf16[1024,1536]{1,0:T(8,128)(2,1)S(1)}, bf16[1024,1536]{1,0:T(8,128)(2,1)}, u32[]{:S(2)}) copy-start(bf16[1024,1536]{1,0:T(8,128)(2,1)} %w_ref.3) | copy-start | bytes 9437188
  2.8 10.9 %collective-permute-start = (bf16[272,1024]{1,0:T(8,128)(2,1)S(1)}, bf16[272,1024]{1,0:T(8,128)(2,1)S(1)}, u32[]{:S(2)}, u32[]{:S(2)}) collective-permute-start(bf16[272,1024]{1,0:T(8,128)(2,1)S(1)} %shard_map.55.own_ref), channel_id=1, source_target_pairs={{0,16},{1,17},{2,18},{3,19},{4,20},{5,21},{6,22},{7,23},{8,24},{9,... | collective-permute-start | bytes 1671176 | tf_op jit(solution)/shard_map/ppermute | solution.py:297
  11.7 13.8 %collective-permute-start.1 = (bf16[272,1024]{1,0:T(8,128)(2,1)S(1)}, bf16[272,1024]{1,0:T(8,128)(2,1)S(1)}, u32[]{:S(2)}, u32[]{:S(2)}) collective-permute-start(bf16[272,1024]{1,0:T(8,128)(2,1)S(1)} %shard_map.55.own_ref), channel_id=1, source_target_pairs={{7,8},{8,7},{15,16},{16,15},{23,24},{24,23},{31,32},{32,31},{39,40... | collective-permute-start | bytes 1671176 | tf_op jit(solution)/shard_map/ppermute | solution.py:298
  16.6 32.5 %all-to-all-start = ((bf16[8,392,256]{2,1,0:T(8,128)(2,1)}), bf16[8,392,256]{2,1,0:T(8,128)(2,1)S(1)}, u32[]{:S(2)}, u32[]{:S(2)}) async-start(bf16[8,392,256]{2,1,0:T(8,128)(2,1)} %get-tuple-element.13.chunk_ref), calls=%async_computation | async-start | bytes 3211264 | tf_op jit(solution)/shard_map/all_to_all | solution.py:317
  25.6 1.9 %copy-start.1 = (bf16[1024,1536]{1,0:T(8,128)(2,1)S(1)}, bf16[1024,1536]{1,0:T(8,128)(2,1)}, u32[]{:S(2)}) copy-start(bf16[1024,1536]{1,0:T(8,128)(2,1)} %w_ref.3) | copy-start | bytes 9437188
  28.3 0.8 %copy-start.3 = (bf16[8,128,256]{2,1,0:T(8,128)(2,1)}, bf16[8,128,256]{2,1,0:T(8,128)(2,1)S(1)}, u32[]{:S(2)}) copy-start(bf16[8,128,256]{2,1,0:T(8,128)(2,1)S(1)} %shard_map.57.edge_ref) | copy-start | bytes 1572868
  29.1 31.9 %collective-permute-start.3 = (bf16[8,128,256]{2,1,0:T(8,128)(2,1)S(1)}, bf16[8,128,256]{2,1,0:T(8,128)(2,1)S(1)}, u32[]{:S(2)}, u32[]{:S(2)}) collective-permute-start(bf16[8,128,256]{2,1,0:T(8,128)(2,1)S(1)} %get-tuple-element.17), channel_id=1, source_target_pairs={{0,32},{1,33},{2,34},{3,35},{4,36},{5,37},{6,38},{7,39},{8,40},{9,... | collective-permute-start | bytes 1572872 | tf_op jit(solution)/shard_map/ppermute | solution.py:330
  37.7 23.3 %collective-permute-start.2 = (bf16[8,128,256]{2,1,0:T(8,128)(2,1)S(1)}, bf16[8,128,256]{2,1,0:T(8,128)(2,1)S(1)}, u32[]{:S(2)}, u32[]{:S(2)}) collective-permute-start(bf16[8,128,256]{2,1,0:T(8,128)(2,1)S(1)} %get-tuple-element.17), channel_id=1, source_target_pairs={{0,8},{1,9},{2,10},{3,11},{4,12},{5,13},{6,14},{7,15},{8,0},{9,1},... | collective-permute-start | bytes 1572872 | tf_op jit(solution)/shard_map/ppermute | solution.py:329
  57.5 16.0 %all-to-all-start.1 = ((bf16[8,136,256]{2,1,0:T(8,128)(2,1)}), bf16[8,136,256]{2,1,0:T(8,128)(2,1)S(1)}, u32[]{:S(2)}, u32[]{:S(2)}) async-start(bf16[8,136,256]{2,1,0:T(8,128)(2,1)} %shard_map.58), calls=%async_computation.1 | async-start | bytes 1114112 | tf_op jit(solution)/shard_map/all_to_all | solution.py:344
  61.0 1.0 %copy-start.4 = (bf16[8,128,256]{2,1,0:T(8,128)(2,1)S(1)}, bf16[8,128,256]{2,1,0:T(8,128)(2,1)}, u32[]{:S(2)}) copy-start(bf16[8,128,256]{2,1,0:T(8,128)(2,1)} %copy-done.3) | copy-start | bytes 1572868
  73.4 3.8 %collective-permute-start.4 = (bf16[8,136,256]{2,1,0:T(8,128)(2,1)S(1)}, bf16[8,136,256]{2,1,0:T(8,128)(2,1)S(1)}, u32[]{:S(2)}, u32[]{:S(2)}) collective-permute-start(bf16[8,136,256]{2,1,0:T(8,128)(2,1)S(1)} %all-to-all-done.1.own_ref), channel_id=1, source_target_pairs={{0,16},{1,17},{2,18},{3,19},{4,20},{5,21},{6,22},{7,23},{8,24},{9,... | collective-permute-start | bytes 1671176 | tf_op jit(solution)/shard_map/ppermute | solution.py:360

commit v4 on v3

--- a/solution.py
+++ b/solution.py
@@ -22,6 +22,7 @@
 SCALE = 1.0 / math.sqrt(HD)
 LOG2E = math.log2(math.e)
 Y_COUNT = 8
+STRIDE = 3
 CORE_BIT = 4
 VMEM_LIMIT = 32 * 1024 * 1024
 
@@ -36,7 +37,7 @@
         y, x_lo, core, x_hi, z = fields(index)
         key = (0, z, x_hi, x_lo) if core == 0 else (1, y, x_hi, x_lo)
         groups.setdefault(key, []).append(index)
-    return [groups[key] for key in sorted(groups)]
+    return [[groups[key][at * STRIDE % HEADS] for at in range(HEADS)] for key in sorted(groups)]
 
 
 def xor_pairs(count, bit):
@@ -73,9 +74,11 @@
 
 
 def key_members(member, core):
-    along_y = (jnp.maximum(member - 1, 0), jnp.minimum(member + 1, HEADS - 1), member ^ 2, member ^ 4)
-    along_z = (member, member ^ 1, member ^ 2, member ^ 4)
-    return [jnp.where(core == 0, one, two) for one, two in zip(along_y, along_z)]
+    place = (member * STRIDE) & (HEADS - 1)
+    along_y = (jnp.maximum(place - 1, 0), jnp.minimum(place + 1, HEADS - 1), place ^ 2, place ^ 4)
+    along_z = (place, place ^ 1, place ^ 2, place ^ 4)
+    places = [jnp.where(core == 0, one, two) for one, two in zip(along_y, along_z)]
+    return [(at * STRIDE) & (HEADS - 1) for at in places]
 
 
 def stack_rows(rows, height, width, kind=jnp.float32):
@@ -320,12 +323,11 @@
         [WHOLE] * 2,
         jax.ShapeDtypeStruct((HEADS, 2 * HD, BLOCK), bf16),
         [],
-        40 * 2 * BLOCK * w_qkv.shape[0] * w_qkv.shape[1],
+        30 * 2 * BLOCK * w_qkv.shape[0] * w_qkv.shape[1],
         4 * 2**20,
         edge,
         w_qkv,
     )
-    keyval, from_edge = lax.optimization_barrier((keyval, from_edge))
     from_x_lo = lax.ppermute(keyval, AXES, xor_pairs(count, 3))
     from_x_hi = lax.ppermute(keyval, AXES, xor_pairs(count, 5))
     held, from_edge = lax.optimization_barrier((held, from_edge))

time: 78.9 us -> 76.4 us (0.968)
  starting transfers between devices: 35.6 us -> 31.3 us
  waiting for transfers between devices: 17.6 us -> 21 us
  local copies, waits for them, and re-layouts: 4.75 us -> 2.93 us
    ppermute x1, starting transfers between devices: 8.64 us -> 4.35 us  [per_device(): from_x_hi = lax.ppermute(keyval, AXES, xor_pairs(count, 5))]
    all_to_all x1, waiting for transfers between devices: 9.32 us -> 13.5 us  [per_device(): lax.all_to_all(chunks, AXES, 0, 0, axis_index_groups=groups, tiled=True)]
    unnamed x10 -> x6, local copies, waits for them, and re-layouts: 4.75 us -> 2.93 us
  transfers between devices with their start and end apart: 7 -> 7, of which waited for: 4 -> 3; matrix products, arithmetic and copies ran while one was open for 0% -> 0% of each run, Pallas kernels for 22% -> 23%
where the time goes in v4:
time: 76.4 us; the launch traced here: 75.9 us
  starting transfers between devices  31.3 us (41%)
  waiting for transfers between devices  21 us (27%)
  Pallas kernels  19.2 us (25%)
  local copies, waits for them, and re-layouts  2.93 us (4%)
  between operations  0.8 us (1%)
    pallas_call x6, Pallas kernels, call(): pl.pallas_call(kernel, in_specs=specs, out_specs=outs or ([WHOLE] * len(s...  19.2 us
    all_to_all x1, waiting for transfers between devices, per_device(): lax.all_to_all(chunks, AXES, 0, 0, axis_index_groups=groups, tiled=True)  13.5 us
    ppermute x1, starting transfers between devices, per_device(): other = lax.ppermute(normed, AXES, xor_pairs(count, CORE_BIT))  8.92 us
    all_to_all x1, starting transfers between devices, per_device(): lax.all_to_all(chunks, AXES, 0, 0, axis_index_groups=groups, tiled=True)  8.68 us
    all_to_all x1, waiting for transfers between devices, per_device(): lax.all_to_all(back, AXES, 0, 0, axis_index_groups=groups, tiled=True)  5.57 us
    ppermute x1, starting transfers between devices, per_device(): from_x_hi = lax.ppermute(keyval, AXES, xor_pairs(count, 5))  4.35 us
    all_to_all x1, starting transfers between devices, per_device(): lax.all_to_all(back, AXES, 0, 0, axis_index_groups=groups, tiled=True)  3.55 us
    unnamed x6, local copies, waits for them, and re-layouts  2.93 us
  transfers between devices with their start and end apart: 7, of which 3 were waited for; matrix products, arithmetic and copies ran while one was open for 0% of the time, Pallas kernels for 23%

profile of v4, /device:TPU:1, one launch (start us, length us, event | category | flops | bytes accessed | tf_op | source)
XLA Modules:
  0.0 75.9 jit_solution(11037459729026071908)
XLA Ops:
  0.7 0.7 pad_maximum_fusion.affine_ref
  1.4 0.0 copy-start.2
  1.4 1.0 %copy-done.2 = bf16[256,1024]{1,0:T(8,128)(2,1)S(1)} copy-done((bf16[256,1024]{1,0:T(8,128)(2,1)S(1)}, bf16[256,1024]{1,0:T(8,128)(2,1)}, u32[]{:S(2)}) %copy-start.2) | copy-done | bytes 524312
  2.4 0.0 copy-start
  2.4 0.4 shard_map.55.own_ref
  2.8 8.9 %collective-permute-start = (bf16[272,1024]{1,0:T(8,128)(2,1)S(1)}, bf16[272,1024]{1,0:T(8,128)(2,1)S(1)}, u32[]{:S(2)}, u32[]{:S(2)}) collective-permute-start(bf16[272,1024]{1,0:T(8,128)(2,1)S(1)} %shard_map.55.own_ref), channel_id=1, source_target_pairs={{0,16},{1,17},{2,18},{3,19},{4,20},{5,21},{6,22},{7,23},{8,24},{9,... | collective-permute-start | bytes 1671176 | tf_op jit(solution)/shard_map/ppermute | solution.py:300
  11.7 1.9 %collective-permute-start.1 = (bf16[272,1024]{1,0:T(8,128)(2,1)S(1)}, bf16[272,1024]{1,0:T(8,128)(2,1)S(1)}, u32[]{:S(2)}, u32[]{:S(2)}) collective-permute-start(bf16[272,1024]{1,0:T(8,128)(2,1)S(1)} %shard_map.55.own_ref), channel_id=1, source_target_pairs={{7,8},{8,7},{15,16},{16,15},{23,24},{24,23},{31,32},{32,31},{39,40... | collective-permute-start | bytes 1671176 | tf_op jit(solution)/shard_map/ppermute | solution.py:301
  13.7 0.0 collective-permute-done.other_ref
  13.7 0.0 copy-done
  13.7 2.9 %shard_map.56 = (bf16[8,392,256]{2,1,0:T(8,128)(2,1)}, bf16[8,128,256]{2,1,0:T(8,128)(2,1)S(1)}) custom-call(s32[1]{0:T(128)} %bitcast.index_ref, s32[1]{0:T(128)S(6)} %copy.6.links_ref, bf16[272,1024]{1,0:T(8,128)(2,1)S(1)} %shard_map.55.own_ref, bf16[272,1024]{1,0:T(8,128)(2,1)S(1)} %collective-permute-done.other_ref, bf16[1024,1536]{1,0:T(8,128)(2,1)S(1)} %copy-done), custom_call_target="tpu_custom_call" | custom-call | flops 32212254720 | bytes 6291456 | tf_op jit(solution)/shard_map/pallas_call | solution.py:271
  16.6 8.7 %all-to-all-start = ((bf16[8,392,256]{2,1,0:T(8,128)(2,1)}), bf16[8,392,256]{2,1,0:T(8,128)(2,1)S(1)}, u32[]{:S(2)}, u32[]{:S(2)}) async-start(bf16[8,392,256]{2,1,0:T(8,128)(2,1)} %get-tuple-element.11.chunk_ref), calls=%async_computation | async-start | bytes 3211264 | tf_op jit(solution)/shard_map/all_to_all | solution.py:320
  25.3 4.3 %collective-permute-start.3 = (bf16[8,128,256]{2,1,0:T(8,128)(2,1)S(1)}, bf16[8,128,256]{2,1,0:T(8,128)(2,1)}, u32[]{:S(2)}, u32[]{:S(2)}) collective-permute-start(bf16[8,128,256]{2,1,0:T(8,128)(2,1)S(1)} %get-tuple-element.13), channel_id=1, source_target_pairs={{0,32},{1,33},{2,34},{3,35},{4,36},{5,37},{6,38},{7,39},{8,40},{9,... | collective-permute-start | bytes 1572872 | tf_op jit(solution)/shard_map/ppermute | solution.py:332
  29.6 2.0 %collective-permute-start.2 = (bf16[8,128,256]{2,1,0:T(8,128)(2,1)S(1)}, bf16[8,128,256]{2,1,0:T(8,128)(2,1)}, u32[]{:S(2)}, u32[]{:S(2)}) collective-permute-start(bf16[8,128,256]{2,1,0:T(8,128)(2,1)S(1)} %get-tuple-element.13), channel_id=1, source_target_pairs={{0,8},{1,9},{2,10},{3,11},{4,12},{5,13},{6,14},{7,15},{8,0},{9,1},... | collective-permute-start | bytes 1572872 | tf_op jit(solution)/shard_map/ppermute | solution.py:331
  31.6 0.0 collective-permute-done.1.normed_ref
  31.6 0.0 copy-start.1
  31.6 1.9 %copy-done.1 = bf16[1024,1536]{1,0:T(8,128)(2,1)S(1)} copy-done((bf16[1024,1536]{1,0:T(8,128)(2,1)S(1)}, bf16[1024,1536]{1,0:T(8,128)(2,1)}, u32[]{:S(2)}) %copy-start.1) | copy-done | bytes 3145752
  33.5 0.8 %shard_map.57.edge_ref = bf16[8,128,256]{2,1,0:T(8,128)(2,1)S(1)} custom-call(bf16[272,1024]{1,0:T(8,128)(2,1)S(1)} %collective-permute-done.1.normed_ref, bf16[1024,1536]{1,0:T(8,128)(2,1)S(1)} %copy-done.1), custom_call_target="tpu_custom_call" | custom-call | flops 24159191040 | bytes 4194304 | tf_op jit(solution)/shard_map/pallas_call | solution.py:271
  34.3 13.5 %all-to-all-done.held_ref = bf16[8,392,256]{2,1,0:T(8,128)(2,1)S(1)} async-done(((bf16[8,392,256]{2,1,0:T(8,128)(2,1)}), bf16[8,392,256]{2,1,0:T(8,128)(2,1)S(1)}, u32[]{:S(2)}, u32[]{:S(2)}) %all-to-all-start) | async-done | bytes 1605664 | tf_op jit(solution)/shard_map/all_to_all | solution.py:320
  47.8 8.4 %shard_map.58 = bf16[8,136,256]{2,1,0:T(8,128)(2,1)} custom-call(s32[1]{0:T(128)} %bitcast.index_ref, bf16[8,392,256]{2,1,0:T(8,128)(2,1)S(1)} %all-to-all-done.held_ref), custom_call_target="tpu_custom_call" | custom-call | flops 85899345920 | bytes 3145728 | tf_op jit(solution)/shard_map/pallas_call | solution.py:271
  56.3 3.5 %all-to-all-start.1 = ((bf16[8,136,256]{2,1,0:T(8,128)(2,1)}), bf16[8,136,256]{2,1,0:T(8,128)(2,1)S(1)}, u32[]{:S(2)}, u32[]{:S(2)}) async-start(bf16[8,136,256]{2,1,0:T(8,128)(2,1)} %shard_map.58), calls=%async_computation.1 | async-start | bytes 1114112 | tf_op jit(solution)/shard_map/all_to_all | solution.py:346
  59.8 0.0 collective-permute-done.3.x_hi_ref
  59.8 0.0 collective-permute-done.2.x_lo_ref
  59.8 5.6 %shard_map.59.home_ref = f32[8,72,256]{2,1,0:T(8,128)S(1)} custom-call(s32[1]{0:T(128)} %bitcast.index_ref, s32[1]{0:T(128)S(6)} %copy.6.links_ref, bf16[8,392,256]{2,1,0:T(8,128)(2,1)} %get-tuple-element.11.chunk_ref, bf16[8,128,256]{2,1,0:T(8,128)(2,1)} %collective-permute-done.2.x_lo_ref, bf16[8,128,256]{2,1,0:T(8,128)(2,1)} %collective-permute-done.3.x_hi_ref, ...), custom_call_target="tpu_custom_call" | custom-call | flops 42949672960 | bytes 4194304 | tf_op jit(solution)/shard_map/pallas_call | solution.py:271
  65.4 5.6 %all-to-all-done.1.own_ref = bf16[8,136,256]{2,1,0:T(8,128)(2,1)S(1)} async-done(((bf16[8,136,256]{2,1,0:T(8,128)(2,1)}), bf16[8,136,256]{2,1,0:T(8,128)(2,1)S(1)}, u32[]{:S(2)}, u32[]{:S(2)}) %all-to-all-start.1) | async-done | bytes 557088 | tf_op jit(solution)/shard_map/all_to_all | solution.py:346
  71.0 1.9 %collective-permute-start.4 = (bf16[8,136,256]{2,1,0:T(8,128)(2,1)S(1)}, bf16[8,136,256]{2,1,0:T(8,128)(2,1)S(1)}, u32[]{:S(2)}, u32[]{:S(2)}) collective-permute-start(bf16[8,136,256]{2,1,0:T(8,128)(2,1)S(1)} %all-to-all-done.1.own_ref), channel_id=1, source_target_pairs={{0,16},{1,17},{2,18},{3,19},{4,20},{5,21},{6,22},{7,23},{8,24},{9,... | collective-permute-start | bytes 1671176 | tf_op jit(solution)/shard_map/ppermute | solution.py:362
  72.9 1.9 %collective-permute-done.4.other_ref = bf16[8,136,256]{2,1,0:T(8,128)(2,1)S(1)} collective-permute-done((bf16[8,136,256]{2,1,0:T(8,128)(2,1)S(1)}, bf16[8,136,256]{2,1,0:T(8,128)(2,1)S(1)}, u32[]{:S(2)}, u32[]{:S(2)}) %collective-permute-start.4) | collective-permute-done | bytes 557088 | tf_op jit(solution)/shard_map/ppermute | solution.py:362
  74.8 1.1 %shard_map.60 = f32[256,512]{1,0:T(8,128)} custom-call(f32[8,72,256]{2,1,0:T(8,128)S(1)} %shard_map.59.home_ref, bf16[8,136,256]{2,1,0:T(8,128)(2,1)S(1)} %all-to-all-done.1.own_ref, bf16[8,136,256]{2,1,0:T(8,128)(2,1)S(1)} %collective-permute-done.4.other_ref), custom_call_target="tpu_custom_call" | custom-call | flops 10000000 | bytes 2097152 | tf_op jit(solution)/shard_map/pallas_call | solution.py:271
Async XLA Ops:
  1.4 1.0 %copy-start.2 = (bf16[256,1024]{1,0:T(8,128)(2,1)S(1)}, bf16[256,1024]{1,0:T(8,128)(2,1)}, u32[]{:S(2)}) copy-start(bf16[256,1024]{1,0:T(8,128)(2,1)} %tokens_ref.1) | copy-start | bytes 1572868
  2.4 11.3 %copy-start = (bf16[1024,1536]{1,0:T(8,128)(2,1)S(1)}, bf16[1024,1536]{1,0:T(8,128)(2,1)}, u32[]{:S(2)}) copy-start(bf16[1024,1536]{1,0:T(8,128)(2,1)} %w_ref.3) | copy-start | bytes 9437188
  2.8 10.9 %collective-permute-start = (bf16[272,1024]{1,0:T(8,128)(2,1)S(1)}, bf16[272,1024]{1,0:T(8,128)(2,1)S(1)}, u32[]{:S(2)}, u32[]{:S(2)}) collective-permute-start(bf16[272,1024]{1,0:T(8,128)(2,1)S(1)} %shard_map.55.own_ref), channel_id=1, source_target_pairs={{0,16},{1,17},{2,18},{3,19},{4,20},{5,21},{6,22},{7,23},{8,24},{9,... | collective-permute-start | bytes 1671176 | tf_op jit(solution)/shard_map/ppermute | solution.py:300
  11.7 19.8 %collective-permute-start.1 = (bf16[272,1024]{1,0:T(8,128)(2,1)S(1)}, bf16[272,1024]{1,0:T(8,128)(2,1)S(1)}, u32[]{:S(2)}, u32[]{:S(2)}) collective-permute-start(bf16[272,1024]{1,0:T(8,128)(2,1)S(1)} %shard_map.55.own_ref), channel_id=1, source_target_pairs={{7,8},{8,7},{15,16},{16,15},{23,24},{24,23},{31,32},{32,31},{39,40... | collective-permute-start | bytes 1671176 | tf_op jit(solution)/shard_map/ppermute | solution.py:301
  16.6 31.2 %all-to-all-start = ((bf16[8,392,256]{2,1,0:T(8,128)(2,1)}), bf16[8,392,256]{2,1,0:T(8,128)(2,1)S(1)}, u32[]{:S(2)}, u32[]{:S(2)}) async-start(bf16[8,392,256]{2,1,0:T(8,128)(2,1)} %get-tuple-element.11.chunk_ref), calls=%async_computation | async-start | bytes 3211264 | tf_op jit(solution)/shard_map/all_to_all | solution.py:320
  25.3 34.6 %collective-permute-start.3 = (bf16[8,128,256]{2,1,0:T(8,128)(2,1)S(1)}, bf16[8,128,256]{2,1,0:T(8,128)(2,1)}, u32[]{:S(2)}, u32[]{:S(2)}) collective-permute-start(bf16[8,128,256]{2,1,0:T(8,128)(2,1)S(1)} %get-tuple-element.13), channel_id=1, source_target_pairs={{0,32},{1,33},{2,34},{3,35},{4,36},{5,37},{6,38},{7,39},{8,40},{9,... | collective-permute-start | bytes 1572872 | tf_op jit(solution)/shard_map/ppermute | solution.py:332
  29.6 30.2 %collective-permute-start.2 = (bf16[8,128,256]{2,1,0:T(8,128)(2,1)S(1)}, bf16[8,128,256]{2,1,0:T(8,128)(2,1)}, u32[]{:S(2)}, u32[]{:S(2)}) collective-permute-start(bf16[8,128,256]{2,1,0:T(8,128)(2,1)S(1)} %get-tuple-element.13), channel_id=1, source_target_pairs={{0,8},{1,9},{2,10},{3,11},{4,12},{5,13},{6,14},{7,15},{8,0},{9,1},... | collective-permute-start | bytes 1572872 | tf_op jit(solution)/shard_map/ppermute | solution.py:331
  31.6 1.9 %copy-start.1 = (bf16[1024,1536]{1,0:T(8,128)(2,1)S(1)}, bf16[1024,1536]{1,0:T(8,128)(2,1)}, u32[]{:S(2)}) copy-start(bf16[1024,1536]{1,0:T(8,128)(2,1)} %w_ref.3) | copy-start | bytes 9437188
  56.3 14.7 %all-to-all-start.1 = ((bf16[8,136,256]{2,1,0:T(8,128)(2,1)}), bf16[8,136,256]{2,1,0:T(8,128)(2,1)S(1)}, u32[]{:S(2)}, u32[]{:S(2)}) async-start(bf16[8,136,256]{2,1,0:T(8,128)(2,1)} %shard_map.58), calls=%async_computation.1 | async-start | bytes 1114112 | tf_op jit(solution)/shard_map/all_to_all | solution.py:346
  71.0 3.8 %collective-permute-start.4 = (bf16[8,136,256]{2,1,0:T(8,128)(2,1)S(1)}, bf16[8,136,256]{2,1,0:T(8,128)(2,1)S(1)}, u32[]{:S(2)}, u32[]{:S(2)}) collective-permute-start(bf16[8,136,256]{2,1,0:T(8,128)(2,1)S(1)} %all-to-all-done.1.own_ref), channel_id=1, source_target_pairs={{0,16},{1,17},{2,18},{3,19},{4,20},{5,21},{6,22},{7,23},{8,24},{9,... | collective-permute-start | bytes 1671176 | tf_op jit(solution)/shard_map/ppermute | solution.py:362

commit v5 on v4

--- a/solution.py
+++ b/solution.py
@@ -217,30 +217,56 @@
         pltpu.make_async_copy(back_ref.at[member], back_hbm.at[member], sems.at[member]).wait()
 
 
-def home_kernel(index_ref, links_ref, chunk_ref, x_lo_ref, x_hi_ref, edge_ref, out_ref, score_ref, weight_ref, count):
+def near_kernel(index_ref, links_ref, chunk_ref, edge_ref, out_ref, score_ref, weight_ref, count):
     index = index_ref[0]
     y = index & 7
     outer = ((y == 0) & (index > 0)) | ((y == Y_COUNT - 1) & (index < count - 1))
-    times = [(links_ref[0] >> bit) & 1 for bit in (4, 3, 5)] + [jnp.where(outer, 1, 0)]
+    times = [(links_ref[0] >> CORE_BIT) & 1, jnp.where(outer, 1, 0)]
     rows = [jnp.full((1, BLOCK), number, jnp.int32).astype(jnp.float32) for number in times]
 
-    def step(pair, carry):
+    def step(group, carry):
         items = []
         load = lambda ref, head, start: lambda: ref[head, start : start + HD, :]
-        for head in (2 * pair, 2 * pair + 1):
+        for local in range(4):
+            head = 4 * group + local
             query = load(chunk_ref, head, 0)
             items.append((query, load(chunk_ref, head, WIDE + HD), load(chunk_ref, head, WIDE + 2 * HD)))
-            for ref in (x_lo_ref, x_hi_ref, edge_ref):
-                items.append((query, load(ref, head, 0), load(ref, head, HD)))
+            items.append((query, load(edge_ref, head, 0), load(edge_ref, head, HD)))
         results = attend_all(items, score_ref, weight_ref)
-        for local in range(2):
-            accum, top, total = merge([results[local * KEYS + entry] + (rows[entry],) for entry in range(KEYS)])
-            head = 2 * pair + local
+        for local in range(4):
+            accum, top, total = merge([results[2 * local + entry] + (rows[entry],) for entry in range(2)])
+            head = 4 * group + local
             out_ref[head, :HD, :] = accum
             out_ref[head, HD:, :] = stack_rows([top, total], 8, BLOCK)
         return carry
 
-    lax.fori_loop(0, HEADS // 2, step, 0)
+    lax.fori_loop(0, HEADS // 4, step, 0)
+
+
+def home_kernel(links_ref, chunk_ref, x_lo_ref, x_hi_ref, near_ref, out_ref, score_ref, weight_ref):
+    times = [(links_ref[0] >> bit) & 1 for bit in (3, 5)]
+    rows = [jnp.full((1, BLOCK), number, jnp.int32).astype(jnp.float32) for number in times]
+
+    def step(group, carry):
+        items = []
+        load = lambda ref, head, start: lambda: ref[head, start : start + HD, :]
+        for local in range(4):
+            head = 4 * group + local
+            for ref in (x_lo_ref, x_hi_ref):
+                items.append((load(chunk_ref, head, 0), load(ref, head, 0), load(ref, head, HD)))
+        results = attend_all(items, score_ref, weight_ref)
+        for local in range(4):
+            head = 4 * group + local
+            near_total = near_ref[head, HD + 1 : HD + 2, :]
+            near = (near_ref[head, :HD, :], near_ref[head, HD : HD + 1, :])
+            accum, top, total = merge([results[2 * local + entry] + (rows[entry],) for entry in range(2)])
+            peak = jnp.maximum(near[1], top)
+            near_factor, factor = jnp.exp2((near[1] - peak) * LOG2E), jnp.exp2((top - peak) * LOG2E)
+            out_ref[head, :HD, :] = near_factor * near[0] + factor * accum
+            out_ref[head, HD:, :] = stack_rows([peak, near_factor * near_total + factor * total], 8, BLOCK)
+        return carry
+
+    lax.fori_loop(0, HEADS // 4, step, 0)
 
 
 def finish_kernel(home_ref, own_ref, other_ref, out_ref):
@@ -330,7 +356,19 @@
     )
     from_x_lo = lax.ppermute(keyval, AXES, xor_pairs(count, 3))
     from_x_hi = lax.ppermute(keyval, AXES, xor_pairs(count, 5))
-    held, from_edge = lax.optimization_barrier((held, from_edge))
+    near = call(
+        functools.partial(near_kernel, count=count),
+        [SMEM] * 2 + [WHOLE] * 2,
+        jax.ShapeDtypeStruct((HEADS, HD + 8, BLOCK), f32),
+        attend_scratch,
+        16 * 4 * BLOCK * BLOCK * 256,
+        4 * 2**20,
+        index,
+        links,
+        chunks,
+        from_edge,
+    )
+    held, near = lax.optimization_barrier((held, near))
     back = call(
         group_kernel,
         [SMEM, WHOLE],
@@ -345,18 +383,17 @@
     )
     mine = lax.all_to_all(back, AXES, 0, 0, axis_index_groups=groups, tiled=True)
     home = call(
-        functools.partial(home_kernel, count=count),
-        [SMEM] * 2 + [WHOLE] * 4,
+        home_kernel,
+        [SMEM] + [WHOLE] * 4,
         jax.ShapeDtypeStruct((HEADS, HD + 8, BLOCK), f32),
         attend_scratch,
         20 * 32 * 4 * BLOCK * BLOCK * 256,
         4 * 2**20,
-        index,
         links,
         chunks,
         from_x_lo,
         from_x_hi,
-        from_edge,
+        near,
     )
     mine, home = lax.optimization_barrier((mine, home))
     theirs = lax.ppermute(mine, AXES, xor_pairs(count, CORE_BIT))

time: 76.4 us -> 76.4 us (level)
  Pallas kernels: 19.2 us -> 20.6 us
  waiting for transfers between devices: 21 us -> 19.6 us
    all_to_all x1, waiting for transfers between devices: 13.5 us -> 10.2 us  [per_device(): lax.all_to_all(chunks, AXES, 0, 0, axis_index_groups=groups, tiled=True)]
    all_to_all x1, waiting for transfers between devices: 5.57 us -> 7.47 us  [per_device(): lax.all_to_all(back, AXES, 0, 0, axis_index_groups=groups, tiled=True)]
    pallas_call x6 -> x7, Pallas kernels: 19.2 us -> 20.6 us  [call(): pl.pallas_call(kernel, in_specs=specs, out_specs=outs or ([WHOLE] * len(s...]
  transfers between devices with their start and end apart: 7 -> 7, of which waited for: 3 -> 3; matrix products, arithmetic and copies ran while one was open for 0% -> 0% of each run, Pallas kernels for 23% -> 25%
where the time goes in v5:
time: 76.4 us; the launch traced here: 75.9 us
  starting transfers between devices  31.3 us (41%)
  Pallas kernels  20.6 us (27%)
  waiting for transfers between devices  19.6 us (26%)
  local copies, waits for them, and re-layouts  2.93 us (4%)
  between operations  0.8 us (1%)
    pallas_call x7, Pallas kernels, call(): pl.pallas_call(kernel, in_specs=specs, out_specs=outs or ([WHOLE] * len(s...  20.6 us
    all_to_all x1, waiting for transfers between devices, per_device(): lax.all_to_all(chunks, AXES, 0, 0, axis_index_groups=groups, tiled=True)  10.2 us
    ppermute x1, starting transfers between devices, per_device(): other = lax.ppermute(normed, AXES, xor_pairs(count, CORE_BIT))  8.92 us
    all_to_all x1, starting transfers between devices, per_device(): lax.all_to_all(chunks, AXES, 0, 0, axis_index_groups=groups, tiled=True)  8.68 us
    all_to_all x1, waiting for transfers between devices, per_device(): lax.all_to_all(back, AXES, 0, 0, axis_index_groups=groups, tiled=True)  7.47 us
    ppermute x1, starting transfers between devices, per_device(): from_x_hi = lax.ppermute(keyval, AXES, xor_pairs(count, 5))  4.35 us
    all_to_all x1, starting transfers between devices, per_device(): lax.all_to_all(back, AXES, 0, 0, axis_index_groups=groups, tiled=True)  3.55 us
    unnamed x6, local copies, waits for them, and re-layouts  2.93 us
  transfers between devices with their start and end apart: 7, of which 3 were waited for; matrix products, arithmetic and copies ran while one was open for 0% of the time, Pallas kernels for 25%

profile of v5, /device:TPU:1, one launch (start us, length us, event | category | flops | bytes accessed | tf_op | source)
XLA Modules:
  0.0 75.9 jit_solution(3878191202842088056)
XLA Ops:
  0.7 0.7 pad_maximum_fusion.affine_ref
  1.4 0.0 copy-start.2
  1.4 1.0 %copy-done.2 = bf16[256,1024]{1,0:T(8,128)(2,1)S(1)} copy-done((bf16[256,1024]{1,0:T(8,128)(2,1)S(1)}, bf16[256,1024]{1,0:T(8,128)(2,1)}, u32[]{:S(2)}) %copy-start.2) | copy-done | bytes 524312
  2.4 0.0 copy-start
  2.4 0.4 shard_map.55.own_ref
  2.8 8.9 %collective-permute-start = (bf16[272,1024]{1,0:T(8,128)(2,1)S(1)}, bf16[272,1024]{1,0:T(8,128)(2,1)S(1)}, u32[]{:S(2)}, u32[]{:S(2)}) collective-permute-start(bf16[272,1024]{1,0:T(8,128)(2,1)S(1)} %shard_map.55.own_ref), channel_id=1, source_target_pairs={{0,16},{1,17},{2,18},{3,19},{4,20},{5,21},{6,22},{7,23},{8,24},{9,... | collective-permute-start | bytes 1671176 | tf_op jit(solution)/shard_map/ppermute | solution.py:326
  11.7 1.9 %collective-permute-start.1 = (bf16[272,1024]{1,0:T(8,128)(2,1)S(1)}, bf16[272,1024]{1,0:T(8,128)(2,1)S(1)}, u32[]{:S(2)}, u32[]{:S(2)}) collective-permute-start(bf16[272,1024]{1,0:T(8,128)(2,1)S(1)} %shard_map.55.own_ref), channel_id=1, source_target_pairs={{7,8},{8,7},{15,16},{16,15},{23,24},{24,23},{31,32},{32,31},{39,40... | collective-permute-start | bytes 1671176 | tf_op jit(solution)/shard_map/ppermute | solution.py:327
  13.7 0.0 collective-permute-done.other_ref
  13.7 0.0 copy-done
  13.7 2.9 %shard_map.56 = (bf16[8,392,256]{2,1,0:T(8,128)(2,1)}, bf16[8,128,256]{2,1,0:T(8,128)(2,1)S(1)}) custom-call(s32[1]{0:T(128)} %bitcast.index_ref, s32[1]{0:T(128)S(6)} %copy.6.links_ref, bf16[272,1024]{1,0:T(8,128)(2,1)S(1)} %shard_map.55.own_ref, bf16[272,1024]{1,0:T(8,128)(2,1)S(1)} %collective-permute-done.other_ref, bf16[1024,1536]{1,0:T(8,128)(2,1)S(1)} %copy-done), custom_call_target="tpu_custom_call" | custom-call | flops 32212254720 | bytes 6291456 | tf_op jit(solution)/shard_map/pallas_call | solution.py:297
  16.6 8.7 %all-to-all-start = ((bf16[8,392,256]{2,1,0:T(8,128)(2,1)}), bf16[8,392,256]{2,1,0:T(8,128)(2,1)S(1)}, u32[]{:S(2)}, u32[]{:S(2)}) async-start(bf16[8,392,256]{2,1,0:T(8,128)(2,1)} %get-tuple-element.11.chunk_ref), calls=%async_computation | async-start | bytes 3211264 | tf_op jit(solution)/shard_map/all_to_all | solution.py:346
  25.3 4.3 %collective-permute-start.3 = (bf16[8,128,256]{2,1,0:T(8,128)(2,1)S(1)}, bf16[8,128,256]{2,1,0:T(8,128)(2,1)}, u32[]{:S(2)}, u32[]{:S(2)}) collective-permute-start(bf16[8,128,256]{2,1,0:T(8,128)(2,1)S(1)} %get-tuple-element.13), channel_id=1, source_target_pairs={{0,32},{1,33},{2,34},{3,35},{4,36},{5,37},{6,38},{7,39},{8,40},{9,... | collective-permute-start | bytes 1572872 | tf_op jit(solution)/shard_map/ppermute | solution.py:358
  29.6 2.0 %collective-permute-start.2 = (bf16[8,128,256]{2,1,0:T(8,128)(2,1)S(1)}, bf16[8,128,256]{2,1,0:T(8,128)(2,1)}, u32[]{:S(2)}, u32[]{:S(2)}) collective-permute-start(bf16[8,128,256]{2,1,0:T(8,128)(2,1)S(1)} %get-tuple-element.13), channel_id=1, source_target_pairs={{0,8},{1,9},{2,10},{3,11},{4,12},{5,13},{6,14},{7,15},{8,0},{9,1},... | collective-permute-start | bytes 1572872 | tf_op jit(solution)/shard_map/ppermute | solution.py:357
  31.6 0.0 collective-permute-done.1.normed_ref
  31.6 0.0 copy-start.1
  31.6 1.9 %copy-done.1 = bf16[1024,1536]{1,0:T(8,128)(2,1)S(1)} copy-done((bf16[1024,1536]{1,0:T(8,128)(2,1)S(1)}, bf16[1024,1536]{1,0:T(8,128)(2,1)}, u32[]{:S(2)}) %copy-start.1) | copy-done | bytes 3145752
  33.5 0.8 %shard_map.57.edge_ref = bf16[8,128,256]{2,1,0:T(8,128)(2,1)S(1)} custom-call(bf16[272,1024]{1,0:T(8,128)(2,1)S(1)} %collective-permute-done.1.normed_ref, bf16[1024,1536]{1,0:T(8,128)(2,1)S(1)} %copy-done.1), custom_call_target="tpu_custom_call" | custom-call | flops 24159191040 | bytes 4194304 | tf_op jit(solution)/shard_map/pallas_call | solution.py:297
  34.3 3.4 %shard_map.58.near_ref = f32[8,72,256]{2,1,0:T(8,128)S(1)} custom-call(s32[1]{0:T(128)} %bitcast.index_ref, s32[1]{0:T(128)S(6)} %copy.6.links_ref, bf16[8,392,256]{2,1,0:T(8,128)(2,1)} %get-tuple-element.11.chunk_ref, bf16[8,128,256]{2,1,0:T(8,128)(2,1)S(1)} %shard_map.57.edge_ref), custom_call_target="tpu_custom_call" | custom-call | flops 1073741824 | bytes 4194304 | tf_op jit(solution)/shard_map/pallas_call | solution.py:297
  37.6 10.2 %all-to-all-done.held_ref = bf16[8,392,256]{2,1,0:T(8,128)(2,1)S(1)} async-done(((bf16[8,392,256]{2,1,0:T(8,128)(2,1)}), bf16[8,392,256]{2,1,0:T(8,128)(2,1)S(1)}, u32[]{:S(2)}, u32[]{:S(2)}) %all-to-all-start) | async-done | bytes 1605664 | tf_op jit(solution)/shard_map/all_to_all | solution.py:346
  47.8 8.4 %shard_map.59 = bf16[8,136,256]{2,1,0:T(8,128)(2,1)} custom-call(s32[1]{0:T(128)} %bitcast.index_ref, bf16[8,392,256]{2,1,0:T(8,128)(2,1)S(1)} %all-to-all-done.held_ref), custom_call_target="tpu_custom_call" | custom-call | flops 85899345920 | bytes 3145728 | tf_op jit(solution)/shard_map/pallas_call | solution.py:297
  56.3 3.5 %all-to-all-start.1 = ((bf16[8,136,256]{2,1,0:T(8,128)(2,1)}), bf16[8,136,256]{2,1,0:T(8,128)(2,1)S(1)}, u32[]{:S(2)}, u32[]{:S(2)}) async-start(bf16[8,136,256]{2,1,0:T(8,128)(2,1)} %shard_map.59), calls=%async_computation.1 | async-start | bytes 1114112 | tf_op jit(solution)/shard_map/all_to_all | solution.py:384
  59.8 0.0 collective-permute-done.3.x_hi_ref
  59.8 0.0 collective-permute-done.2.x_lo_ref
  59.8 3.7 %shard_map.60.home_ref = f32[8,72,256]{2,1,0:T(8,128)S(1)} custom-call(s32[1]{0:T(128)S(6)} %copy.6.links_ref, bf16[8,392,256]{2,1,0:T(8,128)(2,1)} %get-tuple-element.11.chunk_ref, bf16[8,128,256]{2,1,0:T(8,128)(2,1)} %collective-permute-done.2.x_lo_ref, bf16[8,128,256]{2,1,0:T(8,128)(2,1)} %collective-permute-done.3.x_hi_ref, ...), custom_call_target="tpu_custom_call" | custom-call | flops 42949672960 | bytes 4194304 | tf_op jit(solution)/shard_map/pallas_call | solution.py:297
  63.5 7.5 %all-to-all-done.1.own_ref = bf16[8,136,256]{2,1,0:T(8,128)(2,1)S(1)} async-done(((bf16[8,136,256]{2,1,0:T(8,128)(2,1)}), bf16[8,136,256]{2,1,0:T(8,128)(2,1)S(1)}, u32[]{:S(2)}, u32[]{:S(2)}) %all-to-all-start.1) | async-done | bytes 557088 | tf_op jit(solution)/shard_map/all_to_all | solution.py:384
  71.0 1.9 %collective-permute-start.4 = (bf16[8,136,256]{2,1,0:T(8,128)(2,1)S(1)}, bf16[8,136,256]{2,1,0:T(8,128)(2,1)S(1)}, u32[]{:S(2)}, u32[]{:S(2)}) collective-permute-start(bf16[8,136,256]{2,1,0:T(8,128)(2,1)S(1)} %all-to-all-done.1.own_ref), channel_id=1, source_target_pairs={{0,16},{1,17},{2,18},{3,19},{4,20},{5,21},{6,22},{7,23},{8,24},{9,... | collective-permute-start | bytes 1671176 | tf_op jit(solution)/shard_map/ppermute | solution.py:399
  72.9 1.9 %collective-permute-done.4.other_ref = bf16[8,136,256]{2,1,0:T(8,128)(2,1)S(1)} collective-permute-done((bf16[8,136,256]{2,1,0:T(8,128)(2,1)S(1)}, bf16[8,136,256]{2,1,0:T(8,128)(2,1)S(1)}, u32[]{:S(2)}, u32[]{:S(2)}) %collective-permute-start.4) | collective-permute-done | bytes 557088 | tf_op jit(solution)/shard_map/ppermute | solution.py:399
  74.8 1.1 %shard_map.61 = f32[256,512]{1,0:T(8,128)} custom-call(f32[8,72,256]{2,1,0:T(8,128)S(1)} %shard_map.60.home_ref, bf16[8,136,256]{2,1,0:T(8,128)(2,1)S(1)} %all-to-all-done.1.own_ref, bf16[8,136,256]{2,1,0:T(8,128)(2,1)S(1)} %collective-permute-done.4.other_ref), custom_call_target="tpu_custom_call" | custom-call | flops 10000000 | bytes 2097152 | tf_op jit(solution)/shard_map/pallas_call | solution.py:297
Async XLA Ops:
  1.4 1.0 %copy-start.2 = (bf16[256,1024]{1,0:T(8,128)(2,1)S(1)}, bf16[256,1024]{1,0:T(8,128)(2,1)}, u32[]{:S(2)}) copy-start(bf16[256,1024]{1,0:T(8,128)(2,1)} %tokens_ref.1) | copy-start | bytes 1572868
  2.4 11.3 %copy-start = (bf16[1024,1536]{1,0:T(8,128)(2,1)S(1)}, bf16[1024,1536]{1,0:T(8,128)(2,1)}, u32[]{:S(2)}) copy-start(bf16[1024,1536]{1,0:T(8,128)(2,1)} %w_ref.3) | copy-start | bytes 9437188
  2.8 10.9 %collective-permute-start = (bf16[272,1024]{1,0:T(8,128)(2,1)S(1)}, bf16[272,1024]{1,0:T(8,128)(2,1)S(1)}, u32[]{:S(2)}, u32[]{:S(2)}) collective-permute-start(bf16[272,1024]{1,0:T(8,128)(2,1)S(1)} %shard_map.55.own_ref), channel_id=1, source_target_pairs={{0,16},{1,17},{2,18},{3,19},{4,20},{5,21},{6,22},{7,23},{8,24},{9,... | collective-permute-start | bytes 1671176 | tf_op jit(solution)/shard_map/ppermute | solution.py:326
  11.7 19.8 %collective-permute-start.1 = (bf16[272,1024]{1,0:T(8,128)(2,1)S(1)}, bf16[272,1024]{1,0:T(8,128)(2,1)S(1)}, u32[]{:S(2)}, u32[]{:S(2)}) collective-permute-start(bf16[272,1024]{1,0:T(8,128)(2,1)S(1)} %shard_map.55.own_ref), channel_id=1, source_target_pairs={{7,8},{8,7},{15,16},{16,15},{23,24},{24,23},{31,32},{32,31},{39,40... | collective-permute-start | bytes 1671176 | tf_op jit(solution)/shard_map/ppermute | solution.py:327
  16.6 31.2 %all-to-all-start = ((bf16[8,392,256]{2,1,0:T(8,128)(2,1)}), bf16[8,392,256]{2,1,0:T(8,128)(2,1)S(1)}, u32[]{:S(2)}, u32[]{:S(2)}) async-start(bf16[8,392,256]{2,1,0:T(8,128)(2,1)} %get-tuple-element.11.chunk_ref), calls=%async_computation | async-start | bytes 3211264 | tf_op jit(solution)/shard_map/all_to_all | solution.py:346
  25.3 34.6 %collective-permute-start.3 = (bf16[8,128,256]{2,1,0:T(8,128)(2,1)S(1)}, bf16[8,128,256]{2,1,0:T(8,128)(2,1)}, u32[]{:S(2)}, u32[]{:S(2)}) collective-permute-start(bf16[8,128,256]{2,1,0:T(8,128)(2,1)S(1)} %get-tuple-element.13), channel_id=1, source_target_pairs={{0,32},{1,33},{2,34},{3,35},{4,36},{5,37},{6,38},{7,39},{8,40},{9,... | collective-permute-start | bytes 1572872 | tf_op jit(solution)/shard_map/ppermute | solution.py:358
  29.6 30.2 %collective-permute-start.2 = (bf16[8,128,256]{2,1,0:T(8,128)(2,1)S(1)}, bf16[8,128,256]{2,1,0:T(8,128)(2,1)}, u32[]{:S(2)}, u32[]{:S(2)}) collective-permute-start(bf16[8,128,256]{2,1,0:T(8,128)(2,1)S(1)} %get-tuple-element.13), channel_id=1, source_target_pairs={{0,8},{1,9},{2,10},{3,11},{4,12},{5,13},{6,14},{7,15},{8,0},{9,1},... | collective-permute-start | bytes 1572872 | tf_op jit(solution)/shard_map/ppermute | solution.py:357
  31.6 1.9 %copy-start.1 = (bf16[1024,1536]{1,0:T(8,128)(2,1)S(1)}, bf16[1024,1536]{1,0:T(8,128)(2,1)}, u32[]{:S(2)}) copy-start(bf16[1024,1536]{1,0:T(8,128)(2,1)} %w_ref.3) | copy-start | bytes 9437188
  56.3 14.7 %all-to-all-start.1 = ((bf16[8,136,256]{2,1,0:T(8,128)(2,1)}), bf16[8,136,256]{2,1,0:T(8,128)(2,1)S(1)}, u32[]{:S(2)}, u32[]{:S(2)}) async-start(bf16[8,136,256]{2,1,0:T(8,128)(2,1)} %shard_map.59), calls=%async_computation.1 | async-start | bytes 1114112 | tf_op jit(solution)/shard_map/all_to_all | solution.py:384
  71.0 3.8 %collective-permute-start.4 = (bf16[8,136,256]{2,1,0:T(8,128)(2,1)S(1)}, bf16[8,136,256]{2,1,0:T(8,128)(2,1)S(1)}, u32[]{:S(2)}, u32[]{:S(2)}) collective-permute-start(bf16[8,136,256]{2,1,0:T(8,128)(2,1)S(1)} %all-to-all-done.1.own_ref), channel_id=1, source_target_pairs={{0,16},{1,17},{2,18},{3,19},{4,20},{5,21},{6,22},{7,23},{8,24},{9,... | collective-permute-start | bytes 1671176 | tf_op jit(solution)/shard_map/ppermute | solution.py:399
